TPU v7x, 32 devices: a whole 2x2x4 slice. The times are simulated.
32 devices in a mesh: dp: 32 (over z, y, x, core).
Axes of the slice: x: 2, y: 2, z: 4, core: 2. Of those that a mesh axis runs over, the one named last changes fastest.
Arguments:
- tokens: bfloat16 [8192, 896], P('dp'), may hold values from -6 to 6
- attn_weights: bfloat16 [2048, 896], P('dp'), may hold values from -2 to 2
- mlp_weights: bfloat16 [4864, 3, 896], P('dp'), may hold values from -0.1875 to 0.1875
- norm_gains: bfloat16 [2, 896], replicated, may hold values from 0.5 to 1.5
- qkv_bias: bfloat16 [1152], replicated, may hold values from -3 to 3
- seq_lengths: int32 [32, 8], P('dp'), may hold values from 0 to 256, as said below
- cotangent: bfloat16 [8192, 896], P('dp'), may hold values from -6 to 6
Outputs:
- layer_out: bfloat16 [8192, 896], P('dp')
- grad_tokens: float32 [8192, 896], P('dp')
- grad_attn: float32 [2048, 896], P('dp')
- grad_mlp: float32 [4864, 3, 896], P('dp')
- grad_gains: float32 [2, 896], replicated
- grad_bias: float32 [1152], replicated
Inputs may be any that keep to these rules, and one draw needn't show every extreme that they name: `seq_lengths`: the lengths of one device add up to at most 256 and at least 128; its slots beyond that sum are padding. In every draw one device holds a single sequence of exactly 256 tokens.
All inputs are finite; a program needn't handle non-finite values.
Results may differ from a plain program's by a relative error of at most 0.011.
Values may be sent and summed in bfloat16 or wider, within the bound.
A program may use at most 256 MiB of HBM per device.

v0:
```python
import jax
import jax.numpy as jnp
from jax import lax
from jax.sharding import PartitionSpec as P

HEADS = 14
KV_HEADS = 2
HEAD = 64
SEQS_DEV = 8
D = 896
GROUP = 7
QKV = 1152


epsilon = 1e-06
rope_base = 1000000.0
neg_fill = -1e30


def layout(lengths, slot_count):
    slot_index = jnp.arange(slot_count, dtype=jnp.int32)
    seq_ends = jnp.cumsum(lengths)
    seq_starts = seq_ends - lengths
    filled = seq_ends[SEQS_DEV - 1]
    segment = jnp.sum((slot_index[:, None] >= seq_ends[None, :]).astype(jnp.int32), axis=1)
    starts_all = jnp.concatenate([seq_starts, filled[None]])
    which = segment[:, None] == jnp.arange(SEQS_DEV + 1, dtype=jnp.int32)[None, :]
    start_of = jnp.sum(jnp.where(which, starts_all[None, :], 0), axis=1)
    position = slot_index - start_of
    live = slot_index < filled
    return (segment, position, live)


def half_turn(heads):
    middle = heads.shape[-1] // 2
    return jnp.concatenate([-heads[..., middle:], heads[..., :middle]], axis=-1)


def rope_tables(position):
    index = jnp.arange(HEAD // 2, dtype=jnp.float32)
    freqs = rope_base ** (-2.0 * index / HEAD)
    angles = position.astype(jnp.float32)[:, None] * freqs[None, :]
    angles = jnp.concatenate([angles, angles], axis=1)
    return (jnp.cos(angles), jnp.sin(angles))


def rotate(heads, cosine, sine_table):
    return heads * cosine[:, None, :] + half_turn(heads) * sine_table[:, None, :]


def unrotate(grads, cosine, sine_table):
    return grads * cosine[:, None, :] - half_turn(grads * sine_table[:, None, :])


def normalize(values, gain):
    inv_rms = lax.rsqrt(jnp.mean(values * values, axis=-1, keepdims=True) + epsilon)
    return (values * inv_rms * gain[None, :], inv_rms)


def norm_backward(values, gain, inv_rms, upstream):
    scaled = gain[None, :] * upstream
    gain_grad = jnp.sum(upstream * values * inv_rms, axis=0)
    input_grad = inv_rms * scaled - values * inv_rms**3 * jnp.mean(
        scaled * values, axis=-1, keepdims=True
    )
    return (input_grad, gain_grad)


def contract_last(left, right):
    return lax.dot_general(
        left, right, (((1,), (1,)), ((), ())), preferred_element_type=jnp.float32
    )


def contract_first(left, right):
    return lax.dot_general(
        left, right, (((0,), (0,)), ((), ())), preferred_element_type=jnp.float32
    )


def plain_dot(left, right):
    return jnp.dot(left, right, preferred_element_type=jnp.float32)


def body(tokens, attn_weights, mlp_weights, norm_gains, qkv_bias, seq_lengths, cotangent):
    num_rows = tokens.shape[0]
    block_rows = min(512, num_rows)
    num_blocks = num_rows // block_rows
    kv_width = KV_HEADS * HEAD
    segment, position, live = layout(seq_lengths[0], num_rows)
    slot_index = jnp.arange(num_rows, dtype=jnp.int32)
    gains = norm_gains.astype(jnp.float32)
    biases = qkv_bias.astype(jnp.float32)
    inputs = tokens.astype(jnp.float32)
    attention = lax.all_gather(attn_weights, "dp", axis=0, tiled=True)
    normed_one, inv_one = normalize(inputs, gains[0])
    normed_low = normed_one.astype(jnp.bfloat16)
    projected = contract_last(normed_low, attention[:QKV]) + biases[None, :]
    cosine, sine_table = rope_tables(position)
    query_low = rotate(projected[:, :D].reshape(num_rows, HEADS, HEAD), cosine, sine_table).astype(
        jnp.bfloat16
    )
    key_low = rotate(
        projected[:, D : D + kv_width].reshape(num_rows, KV_HEADS, HEAD), cosine, sine_table
    ).astype(jnp.bfloat16)
    value_low = projected[:, D + kv_width :].reshape(num_rows, KV_HEADS, HEAD).astype(jnp.bfloat16)
    query_blocks = query_low.reshape(num_blocks, block_rows, KV_HEADS, GROUP, HEAD)
    segment_blocks = segment.reshape(num_blocks, block_rows)
    slot_blocks = slot_index.reshape(num_blocks, block_rows)

    def block_scores(query_part, segment_part, slot_part):
        allowed = (segment_part[:, None] == segment[None, :]) & (
            slot_index[None, :] <= slot_part[:, None]
        )
        raw_scores = jnp.einsum(
            "qkgh,skh->kgqs", query_part, key_low, preferred_element_type=jnp.float32
        )
        return jnp.where(allowed[None, None], raw_scores * HEAD ** (-0.5), neg_fill)

    def forward_block(item):
        query_part, segment_part, slot_part = item
        scores = block_scores(query_part, segment_part, slot_part)
        row_peak = jnp.max(scores, axis=-1, keepdims=True)
        exponent = jnp.exp(scores - row_peak)
        row_total = jnp.sum(exponent, axis=-1, keepdims=True)
        probs_low = (exponent / row_total).astype(jnp.bfloat16)
        mixed_heads = jnp.einsum(
            "kgqs,skh->qkgh", probs_low, value_low, preferred_element_type=jnp.float32
        )
        return (mixed_heads, (row_peak + jnp.log(row_total))[..., 0])

    head_blocks, log_totals = lax.map(forward_block, (query_blocks, segment_blocks, slot_blocks))
    attended_low = head_blocks.reshape(num_rows, D).astype(jnp.bfloat16)
    hidden = inputs + contract_last(attended_low, attention[QKV:])
    normed_two, inv_two = normalize(hidden, gains[1])
    normed_two_low = normed_two.astype(jnp.bfloat16)
    feedfwd = lax.all_gather(mlp_weights, "dp", axis=0, tiled=True)
    gate_proj = contract_last(normed_two_low, feedfwd[:, 0, :])
    up_proj = contract_last(normed_two_low, feedfwd[:, 1, :])
    gate_sigmoid = jax.nn.sigmoid(gate_proj)
    active_low = (gate_proj * gate_sigmoid * up_proj).astype(jnp.bfloat16)
    layer_out = (hidden + plain_dot(active_low, feedfwd[:, 2, :])).astype(jnp.bfloat16)
    feedfwd = lax.all_gather(mlp_weights, "dp", axis=0, tiled=True)
    upstream = cotangent.astype(jnp.float32) * live.astype(jnp.float32)[:, None]
    upstream_low = upstream.astype(jnp.bfloat16)
    grad_active = contract_last(upstream_low, feedfwd[:, 2, :])
    grad_gate_low = (
        grad_active * up_proj * gate_sigmoid * (1.0 + gate_proj * (1.0 - gate_sigmoid))
    ).astype(jnp.bfloat16)
    grad_up_low = (grad_active * gate_proj * gate_sigmoid).astype(jnp.bfloat16)
    grad_normed_two = plain_dot(grad_gate_low, feedfwd[:, 0, :]) + plain_dot(
        grad_up_low, feedfwd[:, 1, :]
    )
    grad_mid, grad_gain_two = norm_backward(hidden, gains[1], inv_two, grad_normed_two)
    grad_hidden = upstream + grad_mid
    grad_hidden_low = grad_hidden.astype(jnp.bfloat16)
    attention = lax.all_gather(attn_weights, "dp", axis=0, tiled=True)
    grad_out_proj = contract_first(grad_hidden_low, attended_low)
    grad_attended_low = plain_dot(grad_hidden_low, attention[QKV:]).astype(jnp.bfloat16)
    grad_blocks = grad_attended_low.reshape(num_blocks, block_rows, KV_HEADS, GROUP, HEAD)

    def backward_block(carry, item):
        key_grad, value_grad = carry
        query_part, segment_part, slot_part, grad_part, log_part = item
        scores = block_scores(query_part, segment_part, slot_part)
        probs = jnp.exp(scores - log_part[..., None])
        probs_low = probs.astype(jnp.bfloat16)
        value_grad = value_grad + jnp.einsum(
            "kgqs,qkgh->skh", probs_low, grad_part, preferred_element_type=jnp.float32
        )
        grad_probs = jnp.einsum(
            "qkgh,skh->kgqs", grad_part, value_low, preferred_element_type=jnp.float32
        )
        row_inner = jnp.sum(probs * grad_probs, axis=-1, keepdims=True)
        score_grad_low = (probs * (grad_probs - row_inner) * HEAD ** (-0.5)).astype(jnp.bfloat16)
        query_grad = jnp.einsum(
            "kgqs,skh->qkgh", score_grad_low, key_low, preferred_element_type=jnp.float32
        )
        key_grad = key_grad + jnp.einsum(
            "kgqs,qkgh->skh", score_grad_low, query_part, preferred_element_type=jnp.float32
        )
        return ((key_grad, value_grad), query_grad)

    empty_heads = jnp.zeros((num_rows, KV_HEADS, HEAD), jnp.float32)
    (key_grad, value_grad), query_grads = lax.scan(
        backward_block,
        (empty_heads, empty_heads),
        (query_blocks, segment_blocks, slot_blocks, grad_blocks, log_totals),
    )
    query_pre = unrotate(query_grads.reshape(num_rows, HEADS, HEAD), cosine, sine_table)
    key_pre = unrotate(key_grad, cosine, sine_table)
    grad_qkv_low = jnp.concatenate(
        [
            query_pre.reshape(num_rows, D),
            key_pre.reshape(num_rows, kv_width),
            value_grad.reshape(num_rows, kv_width),
        ],
        axis=1,
    ).astype(jnp.bfloat16)
    grad_bias_term = jnp.sum(grad_qkv_low, axis=0, dtype=jnp.float32)
    grad_qkv_weights = contract_first(grad_qkv_low, normed_low)
    grad_normed_one = plain_dot(grad_qkv_low, attention[:QKV])
    grad_input_mid, grad_gain_one = norm_backward(inputs, gains[0], inv_one, grad_normed_one)
    grad_tokens = grad_hidden + grad_input_mid
    grad_attn_term = jnp.concatenate([grad_qkv_weights, grad_out_proj], axis=0)
    owners = lax.axis_size("dp")
    attn_owned = attn_weights.shape[0]
    mlp_owned = mlp_weights.shape[0]
    attn_flat = grad_attn_term.reshape(owners, attn_owned * D)
    mlp_flat = jnp.stack(
        [
            contract_first(grad_gate_low, normed_two_low),
            contract_first(grad_up_low, normed_two_low),
            contract_first(active_low, upstream_low),
        ],
        axis=1,
    ).reshape(owners, mlp_owned * 3 * D)
    joined = jnp.concatenate([attn_flat, mlp_flat], axis=1)
    summed = lax.psum_scatter(joined, "dp", scatter_dimension=0, tiled=True)
    grad_attn = summed[0, : attn_owned * D].reshape(attn_owned, D)
    grad_mlp = summed[0, attn_owned * D :].reshape(mlp_owned, 3, D)
    grad_gains, grad_bias = lax.psum(
        (jnp.stack([grad_gain_one, grad_gain_two]), grad_bias_term), "dp"
    )
    return (layer_out, grad_tokens, grad_attn, grad_mlp, grad_gains, grad_bias)


def solution(mesh):
    placed = (
        P("dp", None),
        P("dp", None),
        P("dp", None, None),
        P(),
        P(),
        P("dp", None),
        P("dp", None),
    )
    return jax.shard_map(
        body,
        mesh=mesh,
        in_specs=placed,
        out_specs=(P("dp", None), P("dp", None), P("dp", None), P("dp", None, None), P(), P()),
        check_vma=False,
    )
```

profile of v0, /device:TPU:0, one launch (start us, length us, event | category | flops | bytes accessed | tf_op | source)
XLA Modules:
  0.0 1439.4 jit_solution(4437354159688252184)
XLA Ops:
  17.0 56.9 %all-gather.3.cloned.1.call-done = bf16[2048,896]{1,0:T(8,128)(2,1)} async-done(((bf16[64,896]{1,0:T(8,128)(2,1)}), bf16[2048,896]{1,0:T(8,128)(2,1)}) %all-gather.3.cloned.1.call-update) | async-done | bytes 3670032 | tf_op jit(solution)/shard_map/all_gather | solution.py:95
  73.9 2.6 convolution_add_fusion
  82.8 152.4 %all-gather.5.cloned.1.call-done = bf16[4864,3,896]{2,0,1:T(8,128)(2,1)} async-done(((bf16[152,3,896]{2,0,1:T(8,128)(2,1)}), bf16[4864,3,896]{2,0,1:T(8,128)(2,1)}) %all-gather.5.cloned.1.call-update) | async-done | bytes 26148880 | tf_op jit(solution)/shard_map/all_gather | solution.py:137
  235.2 5.4 fusion.2
  240.6 8.5 fusion.4
  249.1 9.1 multiply_convert_fusion
  258.2 8.0 fusion.1
  266.3 7.0 multiply_reduce_fusion
  281.3 7.5 broadcast_multiply_fusion
  288.8 7.9 fusion.17
  296.8 7.4 convolution_bitcast_fusion.1
  304.2 7.6 convolution_bitcast_fusion.2
  315.3 7.6 convolution_bitcast_fusion
  322.9 34.6 %pad_maximum_fusion.1 = f32[4864,3,896]{2,0,1:T(8,128)} fusion(f32[4864,1,896]{2,0,1:T(8,128)} %convolution_bitcast_fusion, f32[4864,1,896]{2,0,1:T(8,128)} %convolution_bitcast_fusion.1, f32[4864,1,896]{2,0,1:T(8,128)} %convolution_bitcast_fusion.2), kind=kLoop, calls=%fused_computation.2 | loop fusion | flops 26148864 | bytes 104595456 | tf_op jit(solution)/shard_map/stack | solution.py:210
  357.5 76.5 %copy.58 = f32[4864,3,896]{2,1,0:T(4,128)} copy(f32[4864,3,896]{2,0,1:T(8,128)} %pad_maximum_fusion.1) | data formatting | bytes 104595456 | tf_op jit(solution)/shard_map/stack | solution.py:210
  434.1 80.1 %reshape.241 = f32[32,408576]{1,0:T(8,128)} reshape(f32[4864,3,896]{2,1,0:T(4,128)} %copy.58) | data formatting | bytes 104595456 | tf_op jit(solution)/shard_map/reshape | solution.py:217
  517.2 3.4 pad_maximum_fusion.2
  520.6 6.8 reshape.240
  527.5 40.6 %pad_maximum_fusion = f32[32,465920]{1,0:T(8,128)} fusion(f32[32,408576]{1,0:T(8,128)} %reshape.241, f32[32,57344]{1,0:T(8,128)} %reshape.240), kind=kLoop, calls=%fused_computation.1 | loop fusion | flops 14909440 | bytes 119275520 | tf_op jit(solution)/shard_map/concatenate | solution.py:218
  569.2 3.6 fusion.50
  573.0 40.9 %all-reduce.1 = (f32[2,896]{1,0:T(2,128)}, f32[1152]{0:T(1024)}) all-reduce(f32[2,896]{1,0:T(2,128)S(1)} %pad_maximum_fusion.6, f32[1152]{0:T(1024)S(1)} %convert_reduce_fusion), channel_id=1, replica_groups=mesh['dp'=32] {'dp'}, use_global_device_ids=true, to_apply=%region_13.14 | all-reduce | flops 2944 | bytes 23552 | tf_op jit(solution)/shard_map/psum | solution.py:222
  616.4 8.5 fusion.30
  624.8 780.7 %all-reduce.4.cloned.1.call-done = f32[32,465920]{1,0:T(8,128)} async-done(((f32[32,465920]{1,0:T(8,128)}), f32[32,465920]{1,0:T(8,128)}) %all-reduce.4.cloned.1.call-update) | async-done | bytes 59637776
  1408.4 20.2 %dynamic-slice_reduce_fusion = f32[408576]{0:T(1024)} fusion(f32[32,465920]{1,0:T(8,128)} %all-reduce.4.cloned.1.call-done, u32[]{:T(128)S(6)} %add.97, u32[]{:T(128)S(6)} %convert.19), kind=kLoop, calls=%fused_computation.47 | loop fusion | bytes 3268616 | tf_op jit(solution)/shard_map/slice | solution.py:221
  (132 shorter events, 40.7 us)
Async XLA Ops:
  7.2 66.8 %all-gather.3.cloned.1.call-start = ((), (), s32[]{:S(2)}) async-start(), calls=%async_computation | async-start | bytes 3784704 | tf_op jit(solution)/shard_map/all_gather | solution.py:95
  7.9 227.3 %all-gather.5.cloned.1.call-start = ((), (), s32[]{:S(2)}) async-start(), calls=%async_computation.1 | async-start | bytes 26966016 | tf_op jit(solution)/shard_map/all_gather | solution.py:137
  8.6 1396.9 %all-reduce.4.cloned.1.call-start = ((), (), s32[]{:S(2)}) async-start(), calls=%async_computation.2 | async-start | bytes 119275520
  14.7 61.9 %copy-start.26 = (f32[896]{0:T(1024)}, f32[896]{0:T(1024)S(1)}, u32[]{:S(2)}) copy-start(f32[896]{0:T(1024)S(1)} %get-tuple-element.98) | copy-start | bytes 10756
  16.9 59.7 %copy-start.28 = (f32[256]{0:T(256)}, f32[256]{0:T(256)S(1)}, u32[]{:S(2)}) copy-start(f32[256]{0:T(256)S(1)} %get-tuple-element.115) | copy-start | bytes 3076
  80.1 160.4 %copy-start.19 = (bf16[2,64,7,256]{3,1,2,0:T(8,128)(2,1)}, bf16[2,64,7,256]{3,1,2,0:T(8,128)(2,1)S(1)}, u32[]{:S(2)}) copy-start(bf16[2,64,7,256]{3,1,2,0:T(8,128)(2,1)S(1)} %fusion.31) | copy-start | bytes 1376260
  82.6 190.8 %copy-start.9 = (f32[256,896]{1,0:T(8,128)}, f32[256,896]{1,0:T(8,128)S(1)}, u32[]{:S(2)}) copy-start(f32[256,896]{1,0:T(8,128)S(1)} %get-tuple-element.121) | copy-start | bytes 2752516
  240.6 8.5 copy-start.16
  240.6 8.5 copy-start.30
  258.2 8.1 copy-start.12
  258.2 8.1 copy-start.14
  276.9 3.1 copy-start.1
  281.3 7.5 copy-start.22
  288.8 7.9 copy-start.15
  296.8 7.4 copy-start.13
  304.2 7.6 copy-start.3
  304.2 7.6 copy-start.20
  434.1 80.1 %copy-start.23 = (f32[256,2,32]{0,2,1:T(8,128)S(1)}, f32[256,2,32]{0,2,1:T(8,128)}, u32[]{:S(2)}) copy-start(f32[256,2,32]{0,2,1:T(8,128)} %get-tuple-element.109) | copy-start | bytes 196612
  434.1 81.1 %copy-start.18 = (bf16[2,64,256]{2,1,0:T(8,128)(2,1)S(1)}, bf16[2,64,256]{2,1,0:T(8,128)(2,1)}, u32[]{:S(2)}) copy-start(bf16[2,64,256]{2,1,0:T(8,128)(2,1)} %fusion.39) | copy-start | bytes 196612
  434.1 81.1 %copy-start.27 = (f32[896]{0:T(1024)S(1)}, f32[896]{0:T(1024)}, u32[]{:S(2)}) copy-start(f32[896]{0:T(1024)} %copy-done.26) | copy-start | bytes 10756
  434.1 81.1 %copy-start.29 = (f32[256]{0:T(256)S(1)}, f32[256]{0:T(256)}, u32[]{:S(2)}) copy-start(f32[256]{0:T(256)} %copy-done.28) | copy-start | bytes 3076
  568.1 45.8 %copy-start.4 = (f32[256,896]{1,0:T(8,128)S(1)}, f32[256,896]{1,0:T(8,128)}, u32[]{:S(2)}) copy-start(f32[256,896]{1,0:T(8,128)} %copy-done.2) | copy-start | bytes 2752516
  568.1 45.8 %copy-start.32 = (f32[256]{0:T(256)S(1)}, f32[256]{0:T(256)}, u32[]{:S(2)}) copy-start(f32[256]{0:T(256)} %get-tuple-element.114) | copy-start | bytes 3076
  569.2 47.1 %copy-start.10 = (f32[256,896]{1,0:T(8,128)S(1)}, f32[256,896]{1,0:T(8,128)}, u32[]{:S(2)}) copy-start(f32[256,896]{1,0:T(8,128)} %copy-done.9) | copy-start | bytes 2752516
  (13 other events, 18.6 us)
Sparse Core Ops, SparseCore 0:
  10.9 63.0 all-gather.2
  76.9 158.2 all-gather.4
  568.2 837.2 all-reduce.3
where the time goes:
time: 1450 us; the launch traced here: 1440 us
  waiting for transfers between devices  991 us (68%)
  local copies, waits for them, and re-layouts  197 us (14%)
  matrix products  103 us (7%)
  other arithmetic  92.5 us (6%)
  blocking collectives  40.9 us (3%)
  between operations  14.7 us (1%)
    unnamed x4, waiting for transfers between devices  782 us
    all_gather x1, waiting for transfers between devices, body(): feedfwd = lax.all_gather(mlp_weights, 'dp', axis=0, tiled=True)  152 us
    reshape x1, local copies, waits for them, and re-layouts, body(): mlp_flat = jnp.stack([contract_first(grad_gate_low, normed_two_low), cont...  80.1 us
    another operation x1, local copies, waits for them, and re-layouts, body(): jnp.stack([contract_first(grad_gate_low, normed_two_low), contract_first(...  76.5 us
    all_gather x1, waiting for transfers between devices, body(): attention = lax.all_gather(attn_weights, 'dp', axis=0, tiled=True)  56.9 us
    psum x1, blocking collectives, body(): lax.psum((jnp.stack([grad_gain_one, grad_gain_two]), grad_bias_term), 'dp')  40.9 us
    concatenate x1, other arithmetic, body(): joined = jnp.concatenate([attn_flat, mlp_flat], axis=1)  40.6 us
    another operation x1, other arithmetic, body(): jnp.stack([contract_first(grad_gate_low, normed_two_low), contract_first(...  34.6 us
  transfers between devices with their start and end apart: 3, of which 3 were waited for; matrix products, arithmetic and copies ran while one was open for 2% of the time, Pallas kernels for 0%

commit v1 on v0

v1 whole, which is shorter than its diff:
```python
import jax
import jax.numpy as jnp
from jax import lax
from jax.sharding import PartitionSpec as P

HEADS = 14
KV_HEADS = 2
HEAD = 64
SEQS_DEV = 8
D = 896
GROUP = 7
QKV = 1152


epsilon = 1e-06
rope_base = 1000000.0
neg_fill = -1e30


def layout(lengths, slot_count):
    slot_index = jnp.arange(slot_count, dtype=jnp.int32)
    seq_ends = jnp.cumsum(lengths)
    seq_starts = seq_ends - lengths
    filled = seq_ends[SEQS_DEV - 1]
    segment = jnp.sum((slot_index[:, None] >= seq_ends[None, :]).astype(jnp.int32), axis=1)
    starts_all = jnp.concatenate([seq_starts, filled[None]])
    which = segment[:, None] == jnp.arange(SEQS_DEV + 1, dtype=jnp.int32)[None, :]
    start_of = jnp.sum(jnp.where(which, starts_all[None, :], 0), axis=1)
    position = slot_index - start_of
    live = slot_index < filled
    return (segment, position, live)


def half_turn(heads):
    middle = heads.shape[-1] // 2
    return jnp.concatenate([-heads[..., middle:], heads[..., :middle]], axis=-1)


def rope_tables(position):
    index = jnp.arange(HEAD // 2, dtype=jnp.float32)
    freqs = rope_base ** (-2.0 * index / HEAD)
    angles = position.astype(jnp.float32)[:, None] * freqs[None, :]
    angles = jnp.concatenate([angles, angles], axis=1)
    return (jnp.cos(angles), jnp.sin(angles))


def rotate(heads, cosine, sine_table):
    return heads * cosine[:, None, :] + half_turn(heads) * sine_table[:, None, :]


def unrotate(grads, cosine, sine_table):
    return grads * cosine[:, None, :] - half_turn(grads * sine_table[:, None, :])


def normalize(values, gain):
    inv_rms = lax.rsqrt(jnp.mean(values * values, axis=-1, keepdims=True) + epsilon)
    return (values * inv_rms * gain[None, :], inv_rms)


def norm_backward(values, gain, inv_rms, upstream):
    scaled = gain[None, :] * upstream
    gain_grad = jnp.sum(upstream * values * inv_rms, axis=0)
    input_grad = inv_rms * scaled - values * inv_rms**3 * jnp.mean(
        scaled * values, axis=-1, keepdims=True
    )
    return (input_grad, gain_grad)


def contract_last(left, right):
    return lax.dot_general(
        left, right, (((1,), (1,)), ((), ())), preferred_element_type=jnp.float32
    )


def contract_first(left, right):
    return lax.dot_general(
        left, right, (((0,), (0,)), ((), ())), preferred_element_type=jnp.float32
    )


def plain_dot(left, right):
    return jnp.dot(left, right, preferred_element_type=jnp.float32)


def bits_of(size):
    return size.bit_length() - 1


def swap(value, size, bit):
    return lax.ppermute(value, "dp", [(i, i ^ (1 << bit)) for i in range(size)])


def scatter_sum(parts, order, size, index):
    held = sorted(order, reverse=True)
    last = order[-1]
    for bit in order:
        axis = held.index(bit)
        mine = (index >> bit) & 1
        away = lax.dynamic_index_in_dim(parts, 1 - mine, axis, keepdims=False)
        kept = lax.dynamic_index_in_dim(parts, mine, axis, keepdims=False)
        come = swap(away, size, bit)
        total = kept.astype(jnp.float32) + come.astype(jnp.float32)
        parts = total if bit == last else total.astype(jnp.bfloat16)
        held.remove(bit)
    return parts


def orders_of(size):
    bits = list(range(1, bits_of(size)))
    third = max(1, len(bits) // 4)
    if len(bits) < 3:
        return (bits, bits, bits)
    x_bits, y_bits = bits[:third], bits[third : 2 * third]
    z_bits = bits[2 * third :]
    return (x_bits + y_bits + z_bits, y_bits + x_bits + z_bits, z_bits + x_bits + y_bits)


def total_over(value, size):
    for bit in range(bits_of(size)):
        value = value + swap(value, size, bit)
    return value


def split_rows(value, count, rows):
    return value.reshape((2,) * bits_of(count) + (rows, value.shape[-1]))


def body(tokens, attn_weights, mlp_weights, norm_gains, qkv_bias, seq_lengths, cotangent):
    size = lax.axis_size("dp")
    index = lax.axis_index("dp")
    core = index & 1
    half = size // 2
    same_core = [list(range(0, size, 2)), list(range(1, size, 2))]
    orders = orders_of(size)
    num_rows = tokens.shape[0]
    attn_owned = attn_weights.shape[0]
    mlp_owned = mlp_weights.shape[0]
    kv_width = KV_HEADS * HEAD

    attn_half = lax.all_gather(attn_weights, "dp", axis=0, axis_index_groups=same_core)
    mlp_flat = mlp_weights.reshape(mlp_owned, 3 * D)
    feedfwd = lax.all_gather(
        mlp_flat, "dp", axis=0, axis_index_groups=same_core, tiled=True
    )
    attn_other = swap(attn_half, size, 0)
    attention = jnp.stack(
        [jnp.where(core == 0, attn_half, attn_other), jnp.where(core == 0, attn_other, attn_half)],
        axis=1,
    ).reshape(size * attn_owned, D)
    w_gate, w_up, w_down = feedfwd[:, :D], feedfwd[:, D : 2 * D], feedfwd[:, 2 * D :]

    segment, position, live = layout(seq_lengths[0], num_rows)
    slot_index = jnp.arange(num_rows, dtype=jnp.int32)
    gains = norm_gains.astype(jnp.float32)
    biases = qkv_bias.astype(jnp.float32)
    inputs = tokens.astype(jnp.float32)
    upstream = cotangent.astype(jnp.float32) * live.astype(jnp.float32)[:, None]
    upstream_low = upstream.astype(jnp.bfloat16)
    upstream_two = jnp.concatenate([upstream_low, swap(upstream_low, size, 0)], axis=0)

    normed_one, inv_one = normalize(inputs, gains[0])
    normed_low = normed_one.astype(jnp.bfloat16)
    projected = contract_last(normed_low, attention[:QKV]) + biases[None, :]
    cosine, sine_table = rope_tables(position)
    query_low = rotate(projected[:, :D].reshape(num_rows, HEADS, HEAD), cosine, sine_table).astype(
        jnp.bfloat16
    )
    key_low = rotate(
        projected[:, D : D + kv_width].reshape(num_rows, KV_HEADS, HEAD), cosine, sine_table
    ).astype(jnp.bfloat16)
    value_low = projected[:, D + kv_width :].reshape(num_rows, KV_HEADS, HEAD).astype(jnp.bfloat16)
    query = query_low.reshape(num_rows, KV_HEADS, GROUP, HEAD)
    allowed = (segment[:, None] == segment[None, :]) & (slot_index[None, :] <= slot_index[:, None])
    raw_scores = jnp.einsum("qkgh,skh->kgqs", query, key_low, preferred_element_type=jnp.float32)
    scores = jnp.where(allowed[None, None], raw_scores * HEAD ** (-0.5), neg_fill)
    row_peak = jnp.max(scores, axis=-1, keepdims=True)
    exponent = jnp.exp(scores - row_peak)
    row_total = jnp.sum(exponent, axis=-1, keepdims=True)
    probs = exponent / row_total
    probs_low = probs.astype(jnp.bfloat16)
    mixed_heads = jnp.einsum(
        "kgqs,skh->qkgh", probs_low, value_low, preferred_element_type=jnp.float32
    )
    attended_low = mixed_heads.reshape(num_rows, D).astype(jnp.bfloat16)
    hidden = inputs + contract_last(attended_low, attention[QKV:])
    normed_two, inv_two = normalize(hidden, gains[1])
    normed_two_low = normed_two.astype(jnp.bfloat16)

    normed_pair = jnp.concatenate([normed_two_low, swap(normed_two_low, size, 0)], axis=0)
    gate_proj = contract_last(normed_pair, w_gate)
    up_proj = contract_last(normed_pair, w_up)
    gate_sigmoid = jax.nn.sigmoid(gate_proj)
    active_low = (gate_proj * gate_sigmoid * up_proj).astype(jnp.bfloat16)
    grad_active = contract_last(upstream_two, w_down)
    grad_gate_low = (
        grad_active * up_proj * gate_sigmoid * (1.0 + gate_proj * (1.0 - gate_sigmoid))
    ).astype(jnp.bfloat16)
    grad_up_low = (grad_active * gate_proj * gate_sigmoid).astype(jnp.bfloat16)
    back_pair = plain_dot(grad_gate_low, w_gate) + plain_dot(grad_up_low, w_up)
    grad_normed_two = back_pair[:num_rows] + swap(back_pair[num_rows:], size, 0)
    down_pair = plain_dot(active_low, w_down)
    layer_out = (hidden + (down_pair[:num_rows] + swap(down_pair[num_rows:], size, 0))).astype(
        jnp.bfloat16
    )

    def weight_sum(left, right, order):
        term = contract_first(left, right).astype(jnp.bfloat16)
        return scatter_sum(split_rows(term, half, mlp_owned), order, size, index)

    sum_down = weight_sum(active_low, upstream_two, orders[2])
    sum_gate = weight_sum(grad_gate_low, normed_pair, orders[0])
    sum_up = weight_sum(grad_up_low, normed_pair, orders[1])

    grad_mid, grad_gain_two = norm_backward(hidden, gains[1], inv_two, grad_normed_two)
    grad_hidden = upstream + grad_mid
    grad_hidden_low = grad_hidden.astype(jnp.bfloat16)
    grad_out_proj = contract_first(grad_hidden_low, attended_low).astype(jnp.bfloat16)
    grad_attended_low = plain_dot(grad_hidden_low, attention[QKV:]).astype(jnp.bfloat16)
    grad_part = grad_attended_low.reshape(num_rows, KV_HEADS, GROUP, HEAD)
    value_grad = jnp.einsum(
        "kgqs,qkgh->skh", probs_low, grad_part, preferred_element_type=jnp.float32
    )
    grad_probs = jnp.einsum(
        "qkgh,skh->kgqs", grad_part, value_low, preferred_element_type=jnp.float32
    )
    row_inner = jnp.sum(probs * grad_probs, axis=-1, keepdims=True)
    score_grad_low = (probs * (grad_probs - row_inner) * HEAD ** (-0.5)).astype(jnp.bfloat16)
    query_grad = jnp.einsum(
        "kgqs,skh->qkgh", score_grad_low, key_low, preferred_element_type=jnp.float32
    )
    key_grad = jnp.einsum(
        "kgqs,qkgh->skh", score_grad_low, query, preferred_element_type=jnp.float32
    )
    query_pre = unrotate(query_grad.reshape(num_rows, HEADS, HEAD), cosine, sine_table)
    key_pre = unrotate(key_grad, cosine, sine_table)
    grad_qkv_low = jnp.concatenate(
        [
            query_pre.reshape(num_rows, D),
            key_pre.reshape(num_rows, kv_width),
            value_grad.reshape(num_rows, kv_width),
        ],
        axis=1,
    ).astype(jnp.bfloat16)
    grad_bias_term = jnp.sum(grad_qkv_low, axis=0, dtype=jnp.float32)
    grad_qkv_weights = contract_first(grad_qkv_low, normed_low).astype(jnp.bfloat16)
    grad_normed_one = plain_dot(grad_qkv_low, attention[:QKV])
    grad_input_mid, grad_gain_one = norm_backward(inputs, gains[0], inv_one, grad_normed_one)
    grad_tokens = grad_hidden + grad_input_mid

    attn_term = jnp.concatenate([grad_qkv_weights, grad_out_proj], axis=0)
    edges = (0, 384, 640, D)
    grad_attn = jnp.concatenate(
        [
            scatter_sum(
                split_rows(attn_term[:, left:right], size, attn_owned), [0] + order, size, index
            )
            for left, right, order in zip(edges[:-1], edges[1:], orders)
        ],
        axis=1,
    )
    grad_mlp = jnp.stack([sum_gate, sum_up, sum_down], axis=1)
    small = total_over(jnp.concatenate([grad_gain_one, grad_gain_two, grad_bias_term]), size)
    grad_gains = small[: 2 * D].reshape(2, D)
    return (layer_out, grad_tokens, grad_attn, grad_mlp, grad_gains, small[2 * D :])


def solution(mesh):
    placed = (
        P("dp", None),
        P("dp", None),
        P("dp", None, None),
        P(),
        P(),
        P("dp", None),
        P("dp", None),
    )
    return jax.shard_map(
        body,
        mesh=mesh,
        in_specs=placed,
        out_specs=(P("dp", None), P("dp", None), P("dp", None), P("dp", None, None), P(), P()),
        check_vma=False,
    )
```

time: 1450 us -> 519 us (0.36)
  waiting for transfers between devices: 991 us -> 341 us
  local copies, waits for them, and re-layouts: 197 us -> 26.3 us
  other arithmetic: 92.5 us -> 23 us
  blocking collectives: 40.9 us -> 0 us
  starting transfers between devices: 0.11 us -> 30 us
  matrix products: 103 us -> 74.2 us
    unnamed x4 -> x2, waiting for transfers between devices: 782 us -> 0.7 us
    ppermute x0 -> x37, waiting for transfers between devices: none -> 142 us  [swap(): return lax.ppermute(value, 'dp', [(i, i ^ 1 << bit) for i in range(size)])]
    reshape x2, local copies, waits for them, and re-layouts: 86.9 us -> 2.7 us  [the longest x1 2.1 us: body(): mlp_flat = mlp_weights.reshape(mlp_owned, 3 * D)]
    another operation x5 -> x0, local copies, waits for them, and re-layouts: 79.8 us -> none  [the longest x1 76.5 us: body(): jnp.stack([contract_first(grad_gate_low, normed_two_low), contract_first(...]
    concatenate x2 -> x4, other arithmetic: 44 us -> 1.01 us  [the longest x1 0.7 us: body(): jnp.concatenate([scatter_sum(split_rows(attn_term[:, left:right], size, a...]
    psum x1 -> x0, blocking collectives: 40.9 us -> none  [body(): lax.psum((jnp.stack([grad_gain_one, grad_gain_two]), grad_bias_term), 'dp')]
    another operation x5 -> x10, other arithmetic: 37.3 us -> 5.88 us  [the longest x3 4.08 us: body(): jnp.stack([jnp.where(core == 0, attn_half, attn_other), jnp.where(core ==...]
    ppermute x0 -> x37, starting transfers between devices: none -> 29.9 us  [swap(): return lax.ppermute(value, 'dp', [(i, i ^ 1 << bit) for i in range(size)])]
  transfers between devices with their start and end apart: 3 -> 39, of which waited for: 3 -> 26; matrix products, arithmetic and copies ran while one was open for 2% -> 19% of each run, Pallas kernels for 0% -> 0%
where the time goes in v1:
time: 519 us; the launch traced here: 510 us
  waiting for transfers between devices  341 us (66%)
  matrix products  74.2 us (14%)
  starting transfers between devices  30 us (6%)
  local copies, waits for them, and re-layouts  26.3 us (5%)
  other arithmetic  23 us (4%)
  between operations  15.5 us (3%)
    ppermute x37, waiting for transfers between devices, swap(): return lax.ppermute(value, 'dp', [(i, i ^ 1 << bit) for i in range(size)])  142 us
    all_gather x1, waiting for transfers between devices, body(): lax.all_gather(mlp_flat, 'dp', axis=0, axis_index_groups=same_core, tiled...  136 us
    all_gather x1, waiting for transfers between devices, body(): lax.all_gather(attn_weights, 'dp', axis=0, axis_index_groups=same_core)  62.5 us
    ppermute x37, starting transfers between devices, swap(): return lax.ppermute(value, 'dp', [(i, i ^ 1 << bit) for i in range(size)])  29.9 us
    dot_general x5, matrix products, contract_last(): lax.dot_general(left, right, (((1,), (1,)), ((), ())), preferred_element_...  24.4 us
    dot_general x5, matrix products, contract_first(): lax.dot_general(left, right, (((0,), (0,)), ((), ())), preferred_element_...  13 us
    dot_general x5, matrix products, plain_dot(): return jnp.dot(left, right, preferred_element_type=jnp.float32)  12.1 us
  transfers between devices with their start and end apart: 39, of which 26 were waited for; matrix products, arithmetic and copies ran while one was open for 19% of the time, Pallas kernels for 0%

profile of v1, /device:TPU:0, one launch (start us, length us, event | category | flops | bytes accessed | tf_op | source)
XLA Modules:
  0.0 510.4 jit_solution(5861480910537296522)
XLA Ops:
  10.1 62.5 %all-gather.6.cloned.1.call-done = bf16[1024,896]{1,0:T(8,128)(2,1)} async-done(((bf16[64,896]{1,0:T(8,128)(2,1)}), bf16[1024,896]{1,0:T(8,128)(2,1)}) %all-gather.6.cloned.1.call-update) | async-done | bytes 1835024 | tf_op jit(solution)/shard_map/all_gather | solution.py:140
  95.7 135.8 %all-gather.4.cloned.1.call-done = bf16[2432,2688]{1,0:T(8,128)(2,1)} async-done(((bf16[152,2688]{1,0:T(8,128)(2,1)}), bf16[2432,2688]{1,0:T(8,128)(2,1)}) %all-gather.4.cloned.1.call-update) | async-done | bytes 13074448 | tf_op jit(solution)/shard_map/all_gather | solution.py:142
  231.4 7.6 %fusion.11 = f32[512,2432]{1,0:T(8,128)} fusion(bf16[2432,2688]{1,0:T(8,128)(2,1)} %all-gather.4.cloned.1.call-done, bf16[256,896]{1,0:T(8,128)(2,1)} %collective-permute-done.1, bf16[256,896]{1,0:T(8,128)(2,1)S(1)} %multiply_convert_fusion.3), kind=kOutput, calls=%fused_computation.25 | convolution fusion | flops 2233204736 | bytes 10256384 | tf_op jit(solution)/shard_map/dot_general | solution.py:70
  239.0 5.7 %fusion.5 = f32[512,2432]{1,0:T(8,128)} fusion(bf16[2432,2688]{1,0:T(8,128)(2,1)S(1)} %copy-done.33, bf16[256,896]{1,0:T(8,128)(2,1)} %collective-permute-done.3, bf16[256,896]{1,0:T(8,128)(2,1)S(1)} %fusion.59), kind=kOutput, calls=%fused_computation.19 | convolution fusion | flops 2233204736 | bytes 10256384 | tf_op jit(solution)/shard_map/dot_general | solution.py:70
  244.7 9.4 %multiply_convert_fusion.1 = (bf16[512,2432]{1,0:T(8,128)(2,1)}, bf16[512,2432]{1,0:T(8,128)(2,1)S(1)}, bf16[512,2432]{1,0:T(8,128)(2,1)}) fusion(f32[512,2432]{1,0:T(8,128)} %fusion.5, f32[512,2432]{1,0:T(8,128)} %fusion.11, bf16[2432,2688]{1,0:T(8,128)(2,1)S(1)} %copy-done.33, bf16[256,896]{1,0:T(8,128)(2,1)} %collective-permute-done.1, ...), kind=kOutput, calls=%fused_computation.6 | convolution fusion | flops 2253127680 | bytes 22708224 | tf_op jit(solution)/shard_map/dot_general | solution.py:70
  254.1 4.7 fusion.9
  265.3 3.8 convolution_convert_fusion.2
  274.0 3.8 convolution_convert_fusion.1
  281.3 3.8 convolution_convert_fusion
  294.0 6.6 %fusion.30 = f32[2,64,7,256]{3,1,2,0:T(8,128)S(1)} fusion(bf16[256,2,64,1]{0,2,3,1:T(8,128)(2,1)S(1)} %copy-done.29, f32[2,256,256,7]{2,1,3,0:T(8,128)} %fusion.97, f32[2,7,256,256]{2,3,1,0:T(8,128)} %get-tuple-element.48, f32[2,7,256]{2,1,0:T(8,128)S(1)} %get-tuple-element.47), kind=kOutput, calls=%fused_computation.72 | convolution fusion | flops 123866880 | bytes 8337408 | tf_op jit(solution)/shard_map/kgqs,skh->qkgh/dot_general | solution.py:228
  300.6 7.2 %broadcast_multiply_fusion = (f32[256,2,64]{0,2,1:T(8,128)}, f32[256,2,64]{0,2,1:T(8,128)}) fusion(f32[256,64]{0,1:T(8,128)S(1)} %copy-done.17, bf16[256,2,7,64]{0,3,2,1:T(8,128)(2,1)S(1)} %copy-done.19, f32[2,256,256,7]{2,1,3,0:T(8,128)} %fusion.97, f32[2,7,256,256]{2,3,1,0:T(8,128)} %get-tuple-element.48, f32[2,7,256]{2,1,0:T(8,128)S(1)} %get-tuple-element.47), kind=kOutput, calls=%fused_computation.200 | convolution fusion | flops 123899648 | bytes 8140800 | tf_op jit(solution)/shard_map/kgqs,qkgh->skh/dot_general | solution.py:231
  318.7 3.7 collective-permute-done.33
  327.5 3.7 collective-permute-done.35
  345.2 43.4 %collective-permute-done.11 = bf16[2,2,2,64,256]{4,3,0,1,2:T(8,128)(2,1)S(1)} collective-permute-done((bf16[2,2,2,64,256]{4,3,0,1,2:T(8,128)(2,1)S(1)}, bf16[2,2,2,64,256]{4,3,0,1,2:T(8,128)(2,1)S(1)}, u32[]{:S(2)}, u32[]{:S(2)}) %collective-permute-start.11) | collective-permute-done | bytes 262176 | tf_op jit(solution)/shard_map/ppermute | solution.py:90
  391.7 7.7 %collective-permute-done.12 = bf16[2,2,64,256]{3,2,0,1:T(8,128)(2,1)S(1)} collective-permute-done((bf16[2,2,64,256]{3,2,0,1:T(8,128)(2,1)S(1)}, bf16[2,2,64,256]{3,2,0,1:T(8,128)(2,1)S(1)}, u32[]{:S(2)}, u32[]{:S(2)}) %collective-permute-start.12) | collective-permute-done | bytes 131104 | tf_op jit(solution)/shard_map/ppermute | solution.py:90
  400.9 5.7 %collective-permute-done.17 = bf16[2,2,64,256]{3,2,0,1:T(8,128)(2,1)S(1)} collective-permute-done((bf16[2,2,64,256]{3,2,0,1:T(8,128)(2,1)S(1)}, bf16[2,2,64,256]{3,2,0,1:T(8,128)(2,1)S(1)}, u32[]{:S(2)}, u32[]{:S(2)}) %collective-permute-start.17) | collective-permute-done | bytes 131104 | tf_op jit(solution)/shard_map/ppermute | solution.py:90
  406.7 4.2 collective-permute-done.13
  415.8 4.1 collective-permute-done.14
  420.5 3.8 collective-permute-done.19
  433.1 4.8 collective-permute-done.8
  441.1 4.3 collective-permute-done.9
  449.3 27.9 %collective-permute-done.29 = bf16[2,2,152,896]{3,2,0,1:T(8,128)(2,1)S(1)} collective-permute-done((bf16[2,2,152,896]{3,2,0,1:T(8,128)(2,1)S(1)}, bf16[2,2,152,896]{3,2,0,1:T(8,128)(2,1)S(1)}, u32[]{:S(2)}, u32[]{:S(2)}) %collective-permute-start.29) | collective-permute-done | bytes 1089568 | tf_op jit(solution)/shard_map/ppermute | solution.py:90
  480.5 8.1 %collective-permute-done.26 = bf16[2,152,896]{2,1,0:T(8,128)(2,1)S(1)} collective-permute-done((bf16[2,152,896]{2,1,0:T(8,128)(2,1)S(1)}, bf16[2,152,896]{2,1,0:T(8,128)(2,1)S(1)}, u32[]{:S(2)}, u32[]{:S(2)}) %collective-permute-start.26) | collective-permute-done | bytes 544800 | tf_op jit(solution)/shard_map/ppermute | solution.py:90
  493.5 5.0 collective-permute-done.23
  (272 shorter events, 117.8 us)
Async XLA Ops:
  7.2 65.4 %all-gather.6.cloned.1.call-start = ((), (), s32[]{:S(2)}) async-start(), calls=%async_computation.1 | async-start | bytes 1949696 | tf_op jit(solution)/shard_map/all_gather | solution.py:140
  7.9 223.5 %all-gather.4.cloned.1.call-start = ((), (), s32[]{:S(2)}) async-start(), calls=%async_computation | async-start | bytes 13891584 | tf_op jit(solution)/shard_map/all_gather | solution.py:142
  94.7 144.3 %collective-permute-start.3 = (bf16[256,896]{1,0:T(8,128)(2,1)S(1)}, bf16[256,896]{1,0:T(8,128)(2,1)}, u32[]{:S(2)}, u32[]{:S(2)}) collective-permute-start(bf16[256,896]{1,0:T(8,128)(2,1)S(1)} %fusion.59), channel_id=1, source_target_pairs={{0,1},{1,0},{2,3},{3,2},{4,5},{5,4},{6,7},{7,6},{8,9},{9,8},{10,11... | collective-permute-start | bytes 1376264 | tf_op jit(solution)/shard_map/ppermute | solution.py:90
  261.7 26.7 %collective-permute-start.4 = (f32[256,896]{1,0:T(8,128)S(1)}, f32[256,896]{1,0:T(8,128)S(1)}, u32[]{:S(2)}, u32[]{:S(2)}) collective-permute-start(f32[256,896]{1,0:T(8,128)S(1)} %slice.146), channel_id=1, source_target_pairs={{0,1},{1,0},{2,3},{3,2},{4,5},{5,4},{6,7},{7,6},{8,9},{9,8},{10,11... | collective-permute-start | bytes 2752520 | tf_op jit(solution)/shard_map/ppermute | solution.py:90
  264.7 24.2 %collective-permute-start.2 = (f32[256,896]{1,0:T(8,128)S(1)}, f32[256,896]{1,0:T(8,128)S(1)}, u32[]{:S(2)}, u32[]{:S(2)}) collective-permute-start(f32[256,896]{1,0:T(8,128)S(1)} %slice.144), channel_id=1, source_target_pairs={{0,1},{1,0},{2,3},{3,2},{4,5},{5,4},{6,7},{7,6},{8,9},{9,8},{10,11... | collective-permute-start | bytes 2752520 | tf_op jit(solution)/shard_map/ppermute | solution.py:90
  272.6 152.5 %collective-permute-start.20 = (bf16[2,2,2,152,896]{4,3,0,1,2:T(8,128)(2,1)}, bf16[2,2,2,152,896]{4,3,0,1,2:T(8,128)(2,1)}, u32[]{:S(2)}, u32[]{:S(2)}) collective-permute-start(bf16[2,2,2,152,896]{4,3,0,1,2:T(8,128)(2,1)} %bitcast.287), channel_id=1, source_target_pairs={{0,2},{1,3},{2,0},{3,1},{4,6},{5,7},{6,4},{7,5},{8,10},{9,11},{10,... | collective-permute-start | bytes 6537224 | tf_op jit(solution)/shard_map/ppermute | solution.py:90
  318.7 23.0 %collective-permute-start.5 = (bf16[2,2,2,2,64,384]{5,4,0,1,2,3:T(8,128)(2,1)}, bf16[2,2,2,2,64,384]{5,4,0,1,2,3:T(8,128)(2,1)}, u32[]{:S(2)}, u32[]{:S(2)}) collective-permute-start(bf16[2,2,2,2,64,384]{5,4,0,1,2,3:T(8,128)(2,1)} %bitcast.288), channel_id=1, source_target_pairs={{0,1},{1,0},{2,3},{3,2},{4,5},{5,4},{6,7},{7,6},{8,9},{9,8},{10,11... | collective-permute-start | bytes 2359304 | tf_op jit(solution)/shard_map/ppermute | solution.py:90
  326.1 11.4 %collective-permute-start.10 = (bf16[2,2,2,2,64,256]{5,4,0,1,3,2:T(8,128)(2,1)}, bf16[2,2,2,2,64,256]{5,4,0,1,3,2:T(8,128)(2,1)}, u32[]{:S(2)}, u32[]{:S(2)}) collective-permute-start(bf16[2,2,2,2,64,256]{5,4,0,1,3,2:T(8,128)(2,1)} %bitcast.290), channel_id=1, source_target_pairs={{0,1},{1,0},{2,3},{3,2},{4,5},{5,4},{6,7},{7,6},{8,9},{9,8},{10,11... | collective-permute-start | bytes 1572872 | tf_op jit(solution)/shard_map/ppermute | solution.py:90
  327.0 12.0 %collective-permute-start.15 = (bf16[2,2,2,2,64,256]{5,4,2,3,0,1:T(8,128)(2,1)}, bf16[2,2,2,2,64,256]{5,4,2,3,0,1:T(8,128)(2,1)}, u32[]{:S(2)}, u32[]{:S(2)}) collective-permute-start(bf16[2,2,2,2,64,256]{5,4,2,3,0,1:T(8,128)(2,1)} %bitcast.289), channel_id=1, source_target_pairs={{0,1},{1,0},{2,3},{3,2},{4,5},{5,4},{6,7},{7,6},{8,9},{9,8},{10,11... | collective-permute-start | bytes 1572872 | tf_op jit(solution)/shard_map/ppermute | solution.py:90
  335.8 93.1 %collective-permute-start.24 = (bf16[2,2,2,152,896]{4,3,0,1,2:T(8,128)(2,1)}, bf16[2,2,2,152,896]{4,3,0,1,2:T(8,128)(2,1)S(1)}, u32[]{:S(2)}, u32[]{:S(2)}) collective-permute-start(bf16[2,2,2,152,896]{4,3,0,1,2:T(8,128)(2,1)} %bitcast.286), channel_id=1, source_target_pairs={{0,4},{1,5},{2,6},{3,7},{4,0},{5,1},{6,2},{7,3},{8,12},{9,13},{10,... | collective-permute-start | bytes 6537224 | tf_op jit(solution)/shard_map/ppermute | solution.py:90
  337.6 95.0 %collective-permute-start.28 = (bf16[2,2,2,152,896]{4,3,1,2,0:T(8,128)(2,1)}, bf16[2,2,2,152,896]{4,3,1,2,0:T(8,128)(2,1)S(1)}, u32[]{:S(2)}, u32[]{:S(2)}) collective-permute-start(bf16[2,2,2,152,896]{4,3,1,2,0:T(8,128)(2,1)} %bitcast.302), channel_id=1, source_target_pairs={{0,8},{1,9},{2,10},{3,11},{4,12},{5,13},{6,14},{7,15},{8,0},{9,1},... | collective-permute-start | bytes 6537224 | tf_op jit(solution)/shard_map/ppermute | solution.py:90
  339.0 49.7 %collective-permute-start.11 = (bf16[2,2,2,64,256]{4,3,0,1,2:T(8,128)(2,1)S(1)}, bf16[2,2,2,64,256]{4,3,0,1,2:T(8,128)(2,1)S(1)}, u32[]{:S(2)}, u32[]{:S(2)}) collective-permute-start(bf16[2,2,2,64,256]{4,3,0,1,2:T(8,128)(2,1)S(1)} %dynamic-slice_bitcast_fusion.11), channel_id=1, source_target_pairs={{0,4},{1,5},{2,6},{3,7},{4,0},{5,1},{6,2},{7,3},{8,12},{9,13},{10,... | collective-permute-start | bytes 786440 | tf_op jit(solution)/shard_map/ppermute | solution.py:90
  341.7 48.4 %collective-permute-start.16 = (bf16[2,2,2,64,256]{4,3,1,2,0:T(8,128)(2,1)S(1)}, bf16[2,2,2,64,256]{4,3,1,2,0:T(8,128)(2,1)S(1)}, u32[]{:S(2)}, u32[]{:S(2)}) collective-permute-start(bf16[2,2,2,64,256]{4,3,1,2,0:T(8,128)(2,1)S(1)} %dynamic-slice_bitcast_fusion.10), channel_id=1, source_target_pairs={{0,8},{1,9},{2,10},{3,11},{4,12},{5,13},{6,14},{7,15},{8,0},{9,1},... | collective-permute-start | bytes 786440 | tf_op jit(solution)/shard_map/ppermute | solution.py:90
  388.7 35.6 %collective-permute-start.6 = (bf16[2,2,2,64,384]{4,3,0,1,2:T(8,128)(2,1)S(1)}, bf16[2,2,2,64,384]{4,3,0,1,2:T(8,128)(2,1)S(1)}, u32[]{:S(2)}, u32[]{:S(2)}) collective-permute-start(bf16[2,2,2,64,384]{4,3,0,1,2:T(8,128)(2,1)S(1)} %dynamic-slice_bitcast_fusion.6), channel_id=1, source_target_pairs={{0,2},{1,3},{2,0},{3,1},{4,6},{5,7},{6,4},{7,5},{8,10},{9,11},{10,... | collective-permute-start | bytes 1179656 | tf_op jit(solution)/shard_map/ppermute | solution.py:90
  390.2 9.2 %collective-permute-start.12 = (bf16[2,2,64,256]{3,2,0,1:T(8,128)(2,1)S(1)}, bf16[2,2,64,256]{3,2,0,1:T(8,128)(2,1)S(1)}, u32[]{:S(2)}, u32[]{:S(2)}) collective-permute-start(bf16[2,2,64,256]{3,2,0,1:T(8,128)(2,1)S(1)} %dynamic-slice_bitcast_fusion.14), channel_id=1, source_target_pairs={{0,2},{1,3},{2,0},{3,1},{4,6},{5,7},{6,4},{7,5},{8,10},{9,11},{10,... | collective-permute-start | bytes 393224 | tf_op jit(solution)/shard_map/ppermute | solution.py:90
  427.4 19.1 %collective-permute-start.21 = (bf16[2,2,152,896]{3,2,0,1:T(8,128)(2,1)S(1)}, bf16[2,2,152,896]{3,2,0,1:T(8,128)(2,1)S(1)}, u32[]{:S(2)}, u32[]{:S(2)}) collective-permute-start(bf16[2,2,152,896]{3,2,0,1:T(8,128)(2,1)S(1)} %dynamic-slice_bitcast_fusion.2), channel_id=1, source_target_pairs={{0,4},{1,5},{2,6},{3,7},{4,0},{5,1},{6,2},{7,3},{8,12},{9,13},{10,... | collective-permute-start | bytes 3268616 | tf_op jit(solution)/shard_map/ppermute | solution.py:90
  429.6 17.4 %collective-permute-start.25 = (bf16[2,2,152,896]{3,2,0,1:T(8,128)(2,1)S(1)}, bf16[2,2,152,896]{3,2,0,1:T(8,128)(2,1)S(1)}, u32[]{:S(2)}, u32[]{:S(2)}) collective-permute-start(bf16[2,2,152,896]{3,2,0,1:T(8,128)(2,1)S(1)} %dynamic-slice_bitcast_fusion.1), channel_id=1, source_target_pairs={{0,2},{1,3},{2,0},{3,1},{4,6},{5,7},{6,4},{7,5},{8,10},{9,11},{10,... | collective-permute-start | bytes 3268616 | tf_op jit(solution)/shard_map/ppermute | solution.py:90
  439.1 38.2 %collective-permute-start.29 = (bf16[2,2,152,896]{3,2,0,1:T(8,128)(2,1)S(1)}, bf16[2,2,152,896]{3,2,0,1:T(8,128)(2,1)S(1)}, u32[]{:S(2)}, u32[]{:S(2)}) collective-permute-start(bf16[2,2,152,896]{3,2,0,1:T(8,128)(2,1)S(1)} %dynamic-slice_bitcast_fusion), channel_id=1, source_target_pairs={{0,16},{1,17},{2,18},{3,19},{4,20},{5,21},{6,22},{7,23},{8,24},{9,... | collective-permute-start | bytes 3268616 | tf_op jit(solution)/shard_map/ppermute | solution.py:90
  446.9 33.3 %collective-permute-start.22 = (bf16[2,152,896]{2,1,0:T(8,128)(2,1)S(1)}, bf16[2,152,896]{2,1,0:T(8,128)(2,1)S(1)}, u32[]{:S(2)}, u32[]{:S(2)}) collective-permute-start(bf16[2,152,896]{2,1,0:T(8,128)(2,1)S(1)} %dynamic-slice_bitcast_fusion.5), channel_id=1, source_target_pairs={{0,8},{1,9},{2,10},{3,11},{4,12},{5,13},{6,14},{7,15},{8,0},{9,1},... | collective-permute-start | bytes 1634312 | tf_op jit(solution)/shard_map/ppermute | solution.py:90
  447.3 41.3 %collective-permute-start.26 = (bf16[2,152,896]{2,1,0:T(8,128)(2,1)S(1)}, bf16[2,152,896]{2,1,0:T(8,128)(2,1)S(1)}, u32[]{:S(2)}, u32[]{:S(2)}) collective-permute-start(bf16[2,152,896]{2,1,0:T(8,128)(2,1)S(1)} %dynamic-slice_bitcast_fusion.4), channel_id=1, source_target_pairs={{0,8},{1,9},{2,10},{3,11},{4,12},{5,13},{6,14},{7,15},{8,0},{9,1},... | collective-permute-start | bytes 1634312 | tf_op jit(solution)/shard_map/ppermute | solution.py:90
  477.6 12.1 %collective-permute-start.30 = (bf16[2,152,896]{2,1,0:T(8,128)(2,1)S(1)}, bf16[2,152,896]{2,1,0:T(8,128)(2,1)S(1)}, u32[]{:S(2)}, u32[]{:S(2)}) collective-permute-start(bf16[2,152,896]{2,1,0:T(8,128)(2,1)S(1)} %dynamic-slice_bitcast_fusion.3), channel_id=1, source_target_pairs={{0,2},{1,3},{2,0},{3,1},{4,6},{5,7},{6,4},{7,5},{8,10},{9,11},{10,... | collective-permute-start | bytes 1634312 | tf_op jit(solution)/shard_map/ppermute | solution.py:90
  480.4 18.1 %collective-permute-start.23 = (bf16[152,896]{1,0:T(8,128)(2,1)S(1)}, bf16[152,896]{1,0:T(8,128)(2,1)S(1)}, u32[]{:S(2)}, u32[]{:S(2)}) collective-permute-start(bf16[152,896]{1,0:T(8,128)(2,1)S(1)} %dynamic-slice_bitcast_fusion.9), channel_id=1, source_target_pairs={{0,16},{1,17},{2,18},{3,19},{4,20},{5,21},{6,22},{7,23},{8,24},{9,... | collective-permute-start | bytes 817160 | tf_op jit(solution)/shard_map/ppermute | solution.py:90
  488.7 13.0 %collective-permute-start.27 = (bf16[152,896]{1,0:T(8,128)(2,1)S(1)}, bf16[152,896]{1,0:T(8,128)(2,1)S(1)}, u32[]{:S(2)}, u32[]{:S(2)}) collective-permute-start(bf16[152,896]{1,0:T(8,128)(2,1)S(1)} %dynamic-slice_bitcast_fusion.8), channel_id=1, source_target_pairs={{0,16},{1,17},{2,18},{3,19},{4,20},{5,21},{6,22},{7,23},{8,24},{9,... | collective-permute-start | bytes 817160 | tf_op jit(solution)/shard_map/ppermute | solution.py:90
  489.9 11.8 %collective-permute-start.31 = (bf16[152,896]{1,0:T(8,128)(2,1)S(1)}, bf16[152,896]{1,0:T(8,128)(2,1)S(1)}, u32[]{:S(2)}, u32[]{:S(2)}) collective-permute-start(bf16[152,896]{1,0:T(8,128)(2,1)S(1)} %dynamic-slice_bitcast_fusion.7), channel_id=1, source_target_pairs={{0,4},{1,5},{2,6},{3,7},{4,0},{5,1},{6,2},{7,3},{8,12},{9,13},{10,... | collective-permute-start | bytes 817160 | tf_op jit(solution)/shard_map/ppermute | solution.py:90
  (52 other events, 747.0 us)
Sparse Core Ops, SparseCore 0:
  10.7 61.8 all-gather.5
  75.9 155.5 all-gather.3

commit v2 on v1

--- a/solution.py
+++ b/solution.py
@@ -90,35 +90,23 @@
     return lax.ppermute(value, "dp", [(i, i ^ (1 << bit)) for i in range(size)])
 
 
-def scatter_sum(parts, order, size, index):
-    held = sorted(order, reverse=True)
-    last = order[-1]
-    for bit in order:
-        axis = held.index(bit)
-        mine = (index >> bit) & 1
-        away = lax.dynamic_index_in_dim(parts, 1 - mine, axis, keepdims=False)
-        kept = lax.dynamic_index_in_dim(parts, mine, axis, keepdims=False)
-        come = swap(away, size, bit)
-        total = kept.astype(jnp.float32) + come.astype(jnp.float32)
-        parts = total if bit == last else total.astype(jnp.bfloat16)
-        held.remove(bit)
-    return parts
-
-
 def orders_of(size):
     bits = list(range(1, bits_of(size)))
-    third = max(1, len(bits) // 4)
-    if len(bits) < 3:
-        return (bits, bits, bits)
-    x_bits, y_bits = bits[:third], bits[third : 2 * third]
-    z_bits = bits[2 * third :]
-    return (x_bits + y_bits + z_bits, y_bits + x_bits + z_bits, z_bits + x_bits + y_bits)
-
-
-def total_over(value, size):
-    for bit in range(bits_of(size)):
-        value = value + swap(value, size, bit)
-    return value
+    near, far = bits[:3], bits[3:]
+    return tuple(near[i:] + near[:i] + far for i in range(3))
+
+
+def start_together(values):
+    return list(lax.optimization_barrier(tuple(values)))
+
+
+def take(value, axis, which):
+    return lax.index_in_dim(value, which, axis, keepdims=False)
+
+
+def add_low(kept, come, last):
+    total = kept.astype(jnp.float32) + come.astype(jnp.float32)
+    return total if last else total.astype(jnp.bfloat16)
 
 
 def split_rows(value, count, rows):
@@ -138,16 +126,25 @@
     kv_width = KV_HEADS * HEAD
 
     attn_half = lax.all_gather(attn_weights, "dp", axis=0, axis_index_groups=same_core)
-    mlp_flat = mlp_weights.reshape(mlp_owned, 3 * D)
-    feedfwd = lax.all_gather(
-        mlp_flat, "dp", axis=0, axis_index_groups=same_core, tiled=True
-    )
+    pieces = [mlp_weights[:, i, :] for i in range(3)]
+    held = [[], [], []]
+    steps = len(orders[0])
+    for step in range(steps):
+        if step:
+            pieces = start_together(pieces)
+        if step == steps - 1:
+            attn_half, *pieces = start_together([attn_half] + pieces)
+        for i in range(3):
+            bit = orders[i][steps - 1 - step]
+            come = swap(pieces[i], size, bit)
+            held[i] = sorted(held[i] + [bit], reverse=True)
+            pieces[i] = jnp.stack([pieces[i], come], axis=held[i].index(bit))
+    w_gate, w_up, w_down = [piece.reshape(half * mlp_owned, D) for piece in pieces]
     attn_other = swap(attn_half, size, 0)
     attention = jnp.stack(
         [jnp.where(core == 0, attn_half, attn_other), jnp.where(core == 0, attn_other, attn_half)],
         axis=1,
     ).reshape(size * attn_owned, D)
-    w_gate, w_up, w_down = feedfwd[:, :D], feedfwd[:, D : 2 * D], feedfwd[:, 2 * D :]
 
     segment, position, live = layout(seq_lengths[0], num_rows)
     slot_index = jnp.arange(num_rows, dtype=jnp.int32)
@@ -203,13 +200,32 @@
         jnp.bfloat16
     )
 
-    def weight_sum(left, right, order):
-        term = contract_first(left, right).astype(jnp.bfloat16)
-        return scatter_sum(split_rows(term, half, mlp_owned), order, size, index)
-
-    sum_down = weight_sum(active_low, upstream_two, orders[2])
-    sum_gate = weight_sum(grad_gate_low, normed_pair, orders[0])
-    sum_up = weight_sum(grad_up_low, normed_pair, orders[1])
+    all_bits = list(range(bits_of(size) - 1, 0, -1))
+    mlp_held = [list(all_bits) for _ in range(3)]
+    mlp_parts = [
+        split_rows(contract_first(left, right).astype(jnp.bfloat16), half, mlp_owned)
+        for left, right in (
+            (grad_gate_low, normed_pair),
+            (grad_up_low, normed_pair),
+            (active_low, upstream_two),
+        )
+    ]
+
+    def mlp_sends(step):
+        return [
+            take(mlp_parts[i], mlp_held[i].index(orders[i][step]), 1) for i in range(3)
+        ]
+
+    def mlp_receive(step, comes):
+        for i in range(3):
+            bit = orders[i][step]
+            kept = take(mlp_parts[i], mlp_held[i].index(bit), 0)
+            mlp_held[i].remove(bit)
+            mlp_parts[i] = add_low(kept, comes[i], step == steps - 1)
+
+    first_comes = [
+        swap(away, size, orders[i][0]) for i, away in enumerate(mlp_sends(0))
+    ]
 
     grad_mid, grad_gain_two = norm_backward(hidden, gains[1], inv_two, grad_normed_two)
     grad_hidden = upstream + grad_mid
@@ -249,17 +265,38 @@
 
     attn_term = jnp.concatenate([grad_qkv_weights, grad_out_proj], axis=0)
     edges = (0, 384, 640, D)
-    grad_attn = jnp.concatenate(
-        [
-            scatter_sum(
-                split_rows(attn_term[:, left:right], size, attn_owned), [0] + order, size, index
+    attn_parts = [
+        split_rows(attn_term[:, left:right], size, attn_owned)
+        for left, right in zip(edges[:-1], edges[1:])
+    ]
+    attn_orders = [[0] + order for order in orders]
+    attn_held = [list(all_bits) + [0] for _ in range(3)]
+    small = jnp.concatenate([grad_gain_one, grad_gain_two, grad_bias_term])
+    mlp_receive(0, first_comes)
+    for step in range(steps + 1):
+        sends, keeps = [], []
+        for i in range(3):
+            bit = attn_orders[i][step]
+            axis = attn_held[i].index(bit)
+            mine = (index >> bit) & 1
+            sends.append(lax.dynamic_index_in_dim(attn_parts[i], 1 - mine, axis, keepdims=False))
+            keeps.append(lax.dynamic_index_in_dim(attn_parts[i], mine, axis, keepdims=False))
+            attn_held[i].remove(bit)
+        sends.append(small)
+        if step + 1 < steps:
+            sends += mlp_sends(step + 1)
+        sends = start_together(sends)
+        small = sends[3]
+        comes = [swap(sends[i], size, attn_orders[i][step]) for i in range(3)]
+        small = small + swap(small, size, step)
+        if step + 1 < steps:
+            mlp_receive(
+                step + 1,
+                [swap(sends[4 + i], size, orders[i][step + 1]) for i in range(3)],
             )
-            for left, right, order in zip(edges[:-1], edges[1:], orders)
-        ],
-        axis=1,
-    )
-    grad_mlp = jnp.stack([sum_gate, sum_up, sum_down], axis=1)
-    small = total_over(jnp.concatenate([grad_gain_one, grad_gain_two, grad_bias_term]), size)
+        attn_parts = [add_low(keeps[i], comes[i], step == steps) for i in range(3)]
+    grad_attn = jnp.concatenate(attn_parts, axis=1)
+    grad_mlp = jnp.stack(mlp_parts, axis=1)
     grad_gains = small[: 2 * D].reshape(2, D)
     return (layer_out, grad_tokens, grad_attn, grad_mlp, grad_gains, small[2 * D :])
 

time: 519 us -> 409 us (0.79)
  waiting for transfers between devices: 341 us -> 179 us
  other arithmetic: 23 us -> 47.2 us
  starting transfers between devices: 30 us -> 50.7 us
  local copies, waits for them, and re-layouts: 26.3 us -> 37.6 us
    all_gather x1 -> x0, waiting for transfers between devices: 136 us -> none  [body(): lax.all_gather(mlp_flat, 'dp', axis=0, axis_index_groups=same_core, tiled...]
    all_gather x1, waiting for transfers between devices: 62.5 us -> 0.01 us  [body(): lax.all_gather(attn_weights, 'dp', axis=0, axis_index_groups=same_core)]
    ppermute x37 -> x49, waiting for transfers between devices: 142 us -> 178 us  [swap(): return lax.ppermute(value, 'dp', [(i, i ^ 1 << bit) for i in range(size)])]
    ppermute x37 -> x49, starting transfers between devices: 29.9 us -> 50.7 us  [swap(): return lax.ppermute(value, 'dp', [(i, i ^ 1 << bit) for i in range(size)])]
    another operation x7 -> x19, other arithmetic: 1.8 us -> 19.1 us  [the longest x12 17.2 us: body(): pieces[i] = jnp.stack([pieces[i], come], axis=held[i].index(bit))]
    dynamic_slice x11 -> x5, local copies, waits for them, and re-layouts: 14.5 us -> 4.91 us  [the longest x3 2.72 us: body(): lax.dynamic_index_in_dim(attn_parts[i], 1 - mine, axis, keepdims=False)]
    unnamed x74 -> x95, local copies, waits for them, and re-layouts: 3.98 us -> 13.2 us
    squeeze x21, local copies, waits for them, and re-layouts: 0.79 us -> 7.65 us  [the longest x9 5.94 us: take(): return lax.index_in_dim(value, which, axis, keepdims=False)]
  transfers between devices with their start and end apart: 39 -> 50, of which waited for: 26 -> 27; matrix products, arithmetic and copies ran while one was open for 19% -> 30% of each run, Pallas kernels for 0% -> 0%
where the time goes in v2:
time: 409 us; the launch traced here: 400 us
  waiting for transfers between devices  179 us (44%)
  matrix products  71 us (17%)
  starting transfers between devices  50.7 us (12%)
  other arithmetic  47.2 us (12%)
  local copies, waits for them, and re-layouts  37.6 us (9%)
  between operations  15.3 us (4%)
    ppermute x49, waiting for transfers between devices, swap(): return lax.ppermute(value, 'dp', [(i, i ^ 1 << bit) for i in range(size)])  178 us
    ppermute x49, starting transfers between devices, swap(): return lax.ppermute(value, 'dp', [(i, i ^ 1 << bit) for i in range(size)])  50.7 us
    dot_general x5, matrix products, contract_last(): lax.dot_general(left, right, (((1,), (1,)), ((), ())), preferred_element_...  22.6 us
    another operation x12, other arithmetic, body(): pieces[i] = jnp.stack([pieces[i], come], axis=held[i].index(bit))  17.2 us
    convert_element_type x21, other arithmetic, add_low(): return total if last else total.astype(jnp.bfloat16)  14.7 us
    unnamed x95, local copies, waits for them, and re-layouts  13.2 us
    dot_general x5, matrix products, plain_dot(): return jnp.dot(left, right, preferred_element_type=jnp.float32)  12.9 us
    dot_general x5, matrix products, contract_first(): lax.dot_general(left, right, (((0,), (0,)), ((), ())), preferred_element_...  11.1 us
  transfers between devices with their start and end apart: 50, of which 27 were waited for; matrix products, arithmetic and copies ran while one was open for 30% of the time, Pallas kernels for 0%

profile of v2, /device:TPU:0, one launch (start us, length us, event | category | flops | bytes accessed | tf_op | source)
XLA Modules:
  0.0 400.5 jit_solution(2274673148833786635)
XLA Ops:
  9.1 4.1 %collective-permute-start = (bf16[152,896]{1,0:T(8,128)(2,1)S(1)}, bf16[152,896]{1,0:T(8,128)(2,1)S(1)}, u32[]{:S(2)}, u32[]{:S(2)}) collective-permute-start(bf16[152,896]{1,0:T(8,128)(2,1)S(1)} %get-tuple-element.122), channel_id=1, source_target_pairs={{0,16},{1,17},{2,18},{3,19},{4,20},{5,21},{6,22},{7,23},{8,24},{9,... | collective-permute-start | bytes 817160 | tf_op jit(solution)/shard_map/ppermute | solution.py:90
  16.2 24.3 %collective-permute-done = bf16[152,896]{1,0:T(8,128)(2,1)S(1)} collective-permute-done((bf16[152,896]{1,0:T(8,128)(2,1)S(1)}, bf16[152,896]{1,0:T(8,128)(2,1)S(1)}, u32[]{:S(2)}, u32[]{:S(2)}) %collective-permute-start) | collective-permute-done | bytes 272416 | tf_op jit(solution)/shard_map/ppermute | solution.py:90
  40.6 5.9 %collective-permute-done.1 = bf16[152,896]{1,0:T(8,128)(2,1)S(1)} collective-permute-done((bf16[152,896]{1,0:T(8,128)(2,1)S(1)}, bf16[152,896]{1,0:T(8,128)(2,1)S(1)}, u32[]{:S(2)}, u32[]{:S(2)}) %collective-permute-start.1) | collective-permute-done | bytes 272416 | tf_op jit(solution)/shard_map/ppermute | solution.py:90
  46.5 5.0 %collective-permute-done.2 = bf16[152,896]{1,0:T(8,128)(2,1)S(1)} collective-permute-done((bf16[152,896]{1,0:T(8,128)(2,1)S(1)}, bf16[152,896]{1,0:T(8,128)(2,1)S(1)}, u32[]{:S(2)}, u32[]{:S(2)}) %collective-permute-start.2) | collective-permute-done | bytes 272416 | tf_op jit(solution)/shard_map/ppermute | solution.py:90
  55.3 12.4 %collective-permute-done.3 = bf16[2,152,896]{2,1,0:T(8,128)(2,1)S(1)} collective-permute-done((bf16[2,152,896]{2,1,0:T(8,128)(2,1)S(1)}, bf16[2,152,896]{2,1,0:T(8,128)(2,1)S(1)}, u32[]{:S(2)}, u32[]{:S(2)}) %collective-permute-start.3) | collective-permute-done | bytes 544800 | tf_op jit(solution)/shard_map/ppermute | solution.py:90
  76.6 24.7 %collective-permute-done.6 = bf16[2,2,152,896]{3,2,1,0:T(8,128)(2,1)} collective-permute-done((bf16[2,2,152,896]{3,2,1,0:T(8,128)(2,1)S(1)}, bf16[2,2,152,896]{3,2,1,0:T(8,128)(2,1)}, u32[]{:S(2)}, u32[]{:S(2)}) %collective-permute-start.6) | collective-permute-done | bytes 1089568 | tf_op jit(solution)/shard_map/ppermute | solution.py:90
  126.9 4.1 %fusion.87 = (f32[2,7,256]{2,1,0:T(8,128)S(1)}, f32[2,7,256,256]{2,3,1,0:T(8,128)}) fusion(pred[256,256]{0,1:T(8,128)(4,1)} %fusion.59, bf16[256,2,64,1]{0,2,3,1:T(8,128)(2,1)} %fusion.70, bf16[256,2,7,64]{0,3,2,1:T(8,128)(2,1)} %fusion.41), kind=kOutput, calls=%fused_computation.259 | convolution fusion | flops 121110784 | bytes 4274176 | tf_op jit(solution)/shard_map/sub | solution.py:174
  134.7 29.5 %collective-permute-done.13 = bf16[2,2,2,152,896]{4,3,2,1,0:T(8,128)(2,1)} collective-permute-done((bf16[2,2,2,152,896]{4,3,2,1,0:T(8,128)(2,1)}, bf16[2,2,2,152,896]{4,3,2,1,0:T(8,128)(2,1)}, u32[]{:S(2)}, u32[]{:S(2)}) %collective-permute-start.13) | collective-permute-done | bytes 2179104 | tf_op jit(solution)/shard_map/ppermute | solution.py:90
  172.4 6.3 %fusion.48 = f32[512,2432]{1,0:T(8,128)} fusion(bf16[2432,896]{1,0:T(8,128)(2,1)S(1)} %bitcast.372, bf16[256,896]{1,0:T(8,128)(2,1)} %collective-permute-done.15, bf16[256,896]{1,0:T(8,128)(2,1)} %fusion.44), kind=kOutput, calls=%fused_computation.135 | convolution fusion | flops 2233204736 | bytes 10256384 | tf_op jit(solution)/shard_map/dot_general | solution.py:70
  178.7 5.0 %fusion.81 = f32[512,2432]{1,0:T(8,128)} fusion(bf16[2432,896]{1,0:T(8,128)(2,1)S(1)} %bitcast.374, bf16[256,896]{1,0:T(8,128)(2,1)S(1)} %collective-permute-done.10, bf16[256,896]{1,0:T(8,128)(2,1)S(1)} %multiply_convert_fusion.3), kind=kOutput, calls=%fused_computation.253 | convolution fusion | flops 2233204736 | bytes 10256384 | tf_op jit(solution)/shard_map/dot_general | solution.py:70
  183.6 9.6 %multiply_convert_fusion.1 = (bf16[512,2432]{1,0:T(8,128)(2,1)}, bf16[512,2432]{1,0:T(8,128)(2,1)}, bf16[512,2432]{1,0:T(8,128)(2,1)}) fusion(f32[512,2432]{1,0:T(8,128)} %fusion.48, f32[512,2432]{1,0:T(8,128)} %fusion.81, bf16[2432,896]{1,0:T(8,128)(2,1)S(1)} %bitcast.376, bf16[256,896]{1,0:T(8,128)(2,1)S(1)} %collective-permute-done.10, ...), kind=kOutput, calls=%fused_computation.6 | convolution fusion | flops 2253127680 | bytes 22708224 | tf_op jit(solution)/shard_map/dot_general | solution.py:70
  193.2 4.7 %fusion.89 = f32[512,896]{1,0:T(8,128)S(1)} fusion(bf16[512,2432]{1,0:T(8,128)(2,1)} %get-tuple-element.98, bf16[2432,896]{1,0:T(8,128)(2,1)S(1)} %bitcast.375), kind=kOutput, calls=%fused_computation.261 | convolution fusion | flops 2231369728 | bytes 8683520 | tf_op jit(solution)/shard_map/dot_general | solution.py:82
  218.8 4.0 convolution_convert_fusion
  232.6 7.1 %broadcast_multiply_fusion = (f32[256,2,64]{0,2,1:T(8,128)}, f32[256,2,64]{0,2,1:T(8,128)}) fusion(f32[256,64]{0,1:T(8,128)S(1)} %copy-done.28, bf16[256,2,7,64]{0,3,2,1:T(8,128)(2,1)S(1)} %copy-done.30, f32[2,256,256,7]{2,1,3,0:T(8,128)} %fusion.90, f32[2,7,256,256]{2,3,1,0:T(8,128)} %get-tuple-element.138, f32[2,7,256]{2,1,0:T(8,128)S(1)} %get-tuple-element.137), kind=kOutput, calls=%fused_computation.216 | convolution fusion | flops 123899648 | bytes 8140800 | tf_op jit(solution)/shard_map/kgqs,qkgh->skh/dot_general | solution.py:247
  239.7 6.5 %fusion.18 = f32[2,64,7,256]{3,1,2,0:T(8,128)S(1)} fusion(bf16[256,2,64,1]{0,2,3,1:T(8,128)(2,1)S(1)} %copy-done.36, f32[2,256,256,7]{2,1,3,0:T(8,128)} %fusion.90, f32[2,7,256,256]{2,3,1,0:T(8,128)} %get-tuple-element.138, f32[2,7,256]{2,1,0:T(8,128)S(1)} %get-tuple-element.137), kind=kOutput, calls=%fused_computation.66 | convolution fusion | flops 123866880 | bytes 8337408 | tf_op jit(solution)/shard_map/kgqs,skh->qkgh/dot_general | solution.py:244
  263.5 3.8 collective-permute-done.18
  270.6 4.8 %collective-permute-done.19 = bf16[2,2,2,152,896]{4,3,0,1,2:T(8,128)(2,1)} collective-permute-done((bf16[2,2,2,152,896]{4,3,0,1,2:T(8,128)(2,1)}, bf16[2,2,2,152,896]{4,3,0,1,2:T(8,128)(2,1)}, u32[]{:S(2)}, u32[]{:S(2)}) %collective-permute-start.19) | collective-permute-done | bytes 2179104 | tf_op jit(solution)/shard_map/ppermute | solution.py:90
  289.8 16.7 %collective-permute-done.24 = bf16[2,2,152,896]{3,2,0,1:T(8,128)(2,1)S(1)} collective-permute-done((bf16[2,2,152,896]{3,2,0,1:T(8,128)(2,1)}, bf16[2,2,152,896]{3,2,0,1:T(8,128)(2,1)S(1)}, u32[]{:S(2)}, u32[]{:S(2)}) %collective-permute-start.24) | collective-permute-done | bytes 1089568 | tf_op jit(solution)/shard_map/ppermute | solution.py:90
  327.3 5.2 %collective-permute-done.31 = bf16[2,152,896]{2,1,0:T(8,128)(2,1)S(1)} collective-permute-done((bf16[2,152,896]{2,1,0:T(8,128)(2,1)}, bf16[2,152,896]{2,1,0:T(8,128)(2,1)S(1)}, u32[]{:S(2)}, u32[]{:S(2)}) %collective-permute-start.31) | collective-permute-done | bytes 544800 | tf_op jit(solution)/shard_map/ppermute | solution.py:90
  342.2 3.9 collective-permute-done.36
  357.1 3.7 collective-permute-done.40
  360.9 11.2 %collective-permute-done.47 = bf16[152,896]{1,0:T(8,128)(2,1)S(1)} collective-permute-done((bf16[152,896]{1,0:T(8,128)(2,1)S(1)}, bf16[152,896]{1,0:T(8,128)(2,1)S(1)}, u32[]{:S(2)}, u32[]{:S(2)}) %collective-permute-start.47) | collective-permute-done | bytes 272416 | tf_op jit(solution)/shard_map/ppermute | solution.py:90
  372.1 5.8 %collective-permute-done.46 = bf16[152,896]{1,0:T(8,128)(2,1)S(1)} collective-permute-done((bf16[152,896]{1,0:T(8,128)(2,1)S(1)}, bf16[152,896]{1,0:T(8,128)(2,1)S(1)}, u32[]{:S(2)}, u32[]{:S(2)}) %collective-permute-start.46) | collective-permute-done | bytes 272416 | tf_op jit(solution)/shard_map/ppermute | solution.py:90
  377.9 4.6 %collective-permute-done.45 = bf16[152,896]{1,0:T(8,128)(2,1)S(1)} collective-permute-done((bf16[152,896]{1,0:T(8,128)(2,1)S(1)}, bf16[152,896]{1,0:T(8,128)(2,1)S(1)}, u32[]{:S(2)}, u32[]{:S(2)}) %collective-permute-start.45) | collective-permute-done | bytes 272416 | tf_op jit(solution)/shard_map/ppermute | solution.py:90
  (323 shorter events, 172.4 us)
Async XLA Ops:
  7.2 104.8 %all-gather.3.cloned.1.call-start = ((), (), s32[]{:S(2)}) async-start(), calls=%async_computation | async-start | bytes 1949696 | tf_op jit(solution)/shard_map/all_gather | solution.py:128
  9.1 31.4 %collective-permute-start = (bf16[152,896]{1,0:T(8,128)(2,1)S(1)}, bf16[152,896]{1,0:T(8,128)(2,1)S(1)}, u32[]{:S(2)}, u32[]{:S(2)}) collective-permute-start(bf16[152,896]{1,0:T(8,128)(2,1)S(1)} %get-tuple-element.122), channel_id=1, source_target_pairs={{0,16},{1,17},{2,18},{3,19},{4,20},{5,21},{6,22},{7,23},{8,24},{9,... | collective-permute-start | bytes 817160 | tf_op jit(solution)/shard_map/ppermute | solution.py:90
  13.2 33.2 %collective-permute-start.1 = (bf16[152,896]{1,0:T(8,128)(2,1)S(1)}, bf16[152,896]{1,0:T(8,128)(2,1)S(1)}, u32[]{:S(2)}, u32[]{:S(2)}) collective-permute-start(bf16[152,896]{1,0:T(8,128)(2,1)S(1)} %get-tuple-element.123), channel_id=1, source_target_pairs={{0,16},{1,17},{2,18},{3,19},{4,20},{5,21},{6,22},{7,23},{8,24},{9,... | collective-permute-start | bytes 817160 | tf_op jit(solution)/shard_map/ppermute | solution.py:90
  13.3 38.1 %collective-permute-start.2 = (bf16[152,896]{1,0:T(8,128)(2,1)S(1)}, bf16[152,896]{1,0:T(8,128)(2,1)S(1)}, u32[]{:S(2)}, u32[]{:S(2)}) collective-permute-start(bf16[152,896]{1,0:T(8,128)(2,1)S(1)} %get-tuple-element.124), channel_id=1, source_target_pairs={{0,16},{1,17},{2,18},{3,19},{4,20},{5,21},{6,22},{7,23},{8,24},{9,... | collective-permute-start | bytes 817160 | tf_op jit(solution)/shard_map/ppermute | solution.py:90
  69.7 31.6 %collective-permute-start.6 = (bf16[2,2,152,896]{3,2,1,0:T(8,128)(2,1)S(1)}, bf16[2,2,152,896]{3,2,1,0:T(8,128)(2,1)}, u32[]{:S(2)}, u32[]{:S(2)}) collective-permute-start(bf16[2,2,152,896]{3,2,1,0:T(8,128)(2,1)S(1)} %pad_maximum_fusion.8), channel_id=1, source_target_pairs={{0,4},{1,5},{2,6},{3,7},{4,0},{5,1},{6,2},{7,3},{8,12},{9,13},{10,... | collective-permute-start | bytes 3268616 | tf_op jit(solution)/shard_map/ppermute | solution.py:90
  71.3 34.9 %collective-permute-start.7 = (bf16[2,2,152,896]{3,2,1,0:T(8,128)(2,1)S(1)}, bf16[2,2,152,896]{3,2,1,0:T(8,128)(2,1)}, u32[]{:S(2)}, u32[]{:S(2)}) collective-permute-start(bf16[2,2,152,896]{3,2,1,0:T(8,128)(2,1)S(1)} %pad_maximum_fusion.9), channel_id=1, source_target_pairs={{0,8},{1,9},{2,10},{3,11},{4,12},{5,13},{6,14},{7,15},{8,0},{9,1},... | collective-permute-start | bytes 3268616 | tf_op jit(solution)/shard_map/ppermute | solution.py:90
  71.7 37.4 %collective-permute-start.8 = (bf16[2,2,152,896]{3,2,1,0:T(8,128)(2,1)S(1)}, bf16[2,2,152,896]{3,2,1,0:T(8,128)(2,1)}, u32[]{:S(2)}, u32[]{:S(2)}) collective-permute-start(bf16[2,2,152,896]{3,2,1,0:T(8,128)(2,1)S(1)} %pad_maximum_fusion.10), channel_id=1, source_target_pairs={{0,2},{1,3},{2,0},{3,1},{4,6},{5,7},{6,4},{7,5},{8,10},{9,11},{10,... | collective-permute-start | bytes 3268616 | tf_op jit(solution)/shard_map/ppermute | solution.py:90
  76.6 95.8 %collective-permute-start.15 = (bf16[256,896]{1,0:T(8,128)(2,1)}, bf16[256,896]{1,0:T(8,128)(2,1)}, u32[]{:S(2)}, u32[]{:S(2)}) collective-permute-start(bf16[256,896]{1,0:T(8,128)(2,1)} %fusion.44), channel_id=1, source_target_pairs={{0,1},{1,0},{2,3},{3,2},{4,5},{5,4},{6,7},{7,6},{8,9},{9,8},{10,11... | collective-permute-start | bytes 1376264 | tf_op jit(solution)/shard_map/ppermute | solution.py:90
  114.2 50.1 %collective-permute-start.13 = (bf16[2,2,2,152,896]{4,3,2,1,0:T(8,128)(2,1)}, bf16[2,2,2,152,896]{4,3,2,1,0:T(8,128)(2,1)}, u32[]{:S(2)}, u32[]{:S(2)}) collective-permute-start(bf16[2,2,2,152,896]{4,3,2,1,0:T(8,128)(2,1)} %pad_maximum_fusion.5), channel_id=1, source_target_pairs={{0,8},{1,9},{2,10},{3,11},{4,12},{5,13},{6,14},{7,15},{8,0},{9,1},... | collective-permute-start | bytes 6537224 | tf_op jit(solution)/shard_map/ppermute | solution.py:90
  114.5 52.5 %collective-permute-start.12 = (bf16[2,2,2,152,896]{4,3,2,1,0:T(8,128)(2,1)}, bf16[2,2,2,152,896]{4,3,2,1,0:T(8,128)(2,1)}, u32[]{:S(2)}, u32[]{:S(2)}) collective-permute-start(bf16[2,2,2,152,896]{4,3,2,1,0:T(8,128)(2,1)} %pad_maximum_fusion.4), channel_id=1, source_target_pairs={{0,4},{1,5},{2,6},{3,7},{4,0},{5,1},{6,2},{7,3},{8,12},{9,13},{10,... | collective-permute-start | bytes 6537224 | tf_op jit(solution)/shard_map/ppermute | solution.py:90
  115.4 54.3 %collective-permute-start.11 = (bf16[2,2,2,152,896]{4,3,2,1,0:T(8,128)(2,1)}, bf16[2,2,2,152,896]{4,3,2,1,0:T(8,128)(2,1)}, u32[]{:S(2)}, u32[]{:S(2)}) collective-permute-start(bf16[2,2,2,152,896]{4,3,2,1,0:T(8,128)(2,1)} %pad_maximum_fusion.3), channel_id=1, source_target_pairs={{0,2},{1,3},{2,0},{3,1},{4,6},{5,7},{6,4},{7,5},{8,10},{9,11},{10,... | collective-permute-start | bytes 6537224 | tf_op jit(solution)/shard_map/ppermute | solution.py:90
  134.7 44.0 %collective-permute-start.10 = (bf16[256,896]{1,0:T(8,128)(2,1)S(1)}, bf16[256,896]{1,0:T(8,128)(2,1)S(1)}, u32[]{:S(2)}, u32[]{:S(2)}) collective-permute-start(bf16[256,896]{1,0:T(8,128)(2,1)S(1)} %multiply_convert_fusion.3), channel_id=1, source_target_pairs={{0,1},{1,0},{2,3},{3,2},{4,5},{5,4},{6,7},{7,6},{8,9},{9,8},{10,11... | collective-permute-start | bytes 1376264 | tf_op jit(solution)/shard_map/ppermute | solution.py:90
  200.9 25.6 %collective-permute-start.16 = (f32[256,896]{1,0:T(8,128)S(1)}, f32[256,896]{1,0:T(8,128)S(1)}, u32[]{:S(2)}, u32[]{:S(2)}) collective-permute-start(f32[256,896]{1,0:T(8,128)S(1)} %slice.239), channel_id=1, source_target_pairs={{0,1},{1,0},{2,3},{3,2},{4,5},{5,4},{6,7},{7,6},{8,9},{9,8},{10,11... | collective-permute-start | bytes 2752520 | tf_op jit(solution)/shard_map/ppermute | solution.py:90
  203.9 23.0 %collective-permute-start.14 = (f32[256,896]{1,0:T(8,128)S(1)}, f32[256,896]{1,0:T(8,128)S(1)}, u32[]{:S(2)}, u32[]{:S(2)}) collective-permute-start(f32[256,896]{1,0:T(8,128)S(1)} %slice.237), channel_id=1, source_target_pairs={{0,1},{1,0},{2,3},{3,2},{4,5},{5,4},{6,7},{7,6},{8,9},{9,8},{10,11... | collective-permute-start | bytes 2752520 | tf_op jit(solution)/shard_map/ppermute | solution.py:90
  210.4 49.6 %collective-permute-start.17 = (bf16[2,2,2,152,896]{4,3,0,1,2:T(8,128)(2,1)}, bf16[2,2,2,152,896]{4,3,0,1,2:T(8,128)(2,1)}, u32[]{:S(2)}, u32[]{:S(2)}) collective-permute-start(bf16[2,2,2,152,896]{4,3,0,1,2:T(8,128)(2,1)} %bitcast.363), channel_id=1, source_target_pairs={{0,2},{1,3},{2,0},{3,1},{4,6},{5,7},{6,4},{7,5},{8,10},{9,11},{10,... | collective-permute-start | bytes 6537224 | tf_op jit(solution)/shard_map/ppermute | solution.py:90
  218.0 49.4 %collective-permute-start.18 = (bf16[2,2,2,152,896]{4,3,0,2,1:T(8,128)(2,1)}, bf16[2,2,2,152,896]{4,3,0,2,1:T(8,128)(2,1)}, u32[]{:S(2)}, u32[]{:S(2)}) collective-permute-start(bf16[2,2,2,152,896]{4,3,0,2,1:T(8,128)(2,1)} %bitcast.362), channel_id=1, source_target_pairs={{0,4},{1,5},{2,6},{3,7},{4,0},{5,1},{6,2},{7,3},{8,12},{9,13},{10,... | collective-permute-start | bytes 6537224 | tf_op jit(solution)/shard_map/ppermute | solution.py:90
  226.1 49.4 %collective-permute-start.19 = (bf16[2,2,2,152,896]{4,3,0,1,2:T(8,128)(2,1)}, bf16[2,2,2,152,896]{4,3,0,1,2:T(8,128)(2,1)}, u32[]{:S(2)}, u32[]{:S(2)}) collective-permute-start(bf16[2,2,2,152,896]{4,3,0,1,2:T(8,128)(2,1)} %bitcast.361), channel_id=1, source_target_pairs={{0,8},{1,9},{2,10},{3,11},{4,12},{5,13},{6,14},{7,15},{8,0},{9,1},... | collective-permute-start | bytes 6537224 | tf_op jit(solution)/shard_map/ppermute | solution.py:90
  280.4 26.2 %collective-permute-start.24 = (bf16[2,2,152,896]{3,2,0,1:T(8,128)(2,1)}, bf16[2,2,152,896]{3,2,0,1:T(8,128)(2,1)S(1)}, u32[]{:S(2)}, u32[]{:S(2)}) collective-permute-start(bf16[2,2,152,896]{3,2,0,1:T(8,128)(2,1)} %slice_bitcast_fusion.5), channel_id=1, source_target_pairs={{0,4},{1,5},{2,6},{3,7},{4,0},{5,1},{6,2},{7,3},{8,12},{9,13},{10,... | collective-permute-start | bytes 3268616 | tf_op jit(solution)/shard_map/ppermute | solution.py:90
  281.7 27.0 %collective-permute-start.25 = (bf16[2,2,152,896]{3,2,0,1:T(8,128)(2,1)}, bf16[2,2,152,896]{3,2,0,1:T(8,128)(2,1)S(1)}, u32[]{:S(2)}, u32[]{:S(2)}) collective-permute-start(bf16[2,2,152,896]{3,2,0,1:T(8,128)(2,1)} %slice_bitcast_fusion.4), channel_id=1, source_target_pairs={{0,8},{1,9},{2,10},{3,11},{4,12},{5,13},{6,14},{7,15},{8,0},{9,1},... | collective-permute-start | bytes 3268616 | tf_op jit(solution)/shard_map/ppermute | solution.py:90
  282.0 27.8 %collective-permute-start.26 = (bf16[2,2,152,896]{3,2,0,1:T(8,128)(2,1)}, bf16[2,2,152,896]{3,2,0,1:T(8,128)(2,1)S(1)}, u32[]{:S(2)}, u32[]{:S(2)}) collective-permute-start(bf16[2,2,152,896]{3,2,0,1:T(8,128)(2,1)} %slice_bitcast_fusion.3), channel_id=1, source_target_pairs={{0,2},{1,3},{2,0},{3,1},{4,6},{5,7},{6,4},{7,5},{8,10},{9,11},{10,... | collective-permute-start | bytes 3268616 | tf_op jit(solution)/shard_map/ppermute | solution.py:90
  348.5 23.5 %collective-permute-start.47 = (bf16[152,896]{1,0:T(8,128)(2,1)S(1)}, bf16[152,896]{1,0:T(8,128)(2,1)S(1)}, u32[]{:S(2)}, u32[]{:S(2)}) collective-permute-start(bf16[152,896]{1,0:T(8,128)(2,1)S(1)} %slice_bitcast_fusion.15), channel_id=1, source_target_pairs={{0,16},{1,17},{2,18},{3,19},{4,20},{5,21},{6,22},{7,23},{8,24},{9,... | collective-permute-start | bytes 817160 | tf_op jit(solution)/shard_map/ppermute | solution.py:90
  352.2 25.7 %collective-permute-start.46 = (bf16[152,896]{1,0:T(8,128)(2,1)S(1)}, bf16[152,896]{1,0:T(8,128)(2,1)S(1)}, u32[]{:S(2)}, u32[]{:S(2)}) collective-permute-start(bf16[152,896]{1,0:T(8,128)(2,1)S(1)} %slice_bitcast_fusion.16), channel_id=1, source_target_pairs={{0,16},{1,17},{2,18},{3,19},{4,20},{5,21},{6,22},{7,23},{8,24},{9,... | collective-permute-start | bytes 817160 | tf_op jit(solution)/shard_map/ppermute | solution.py:90
  352.2 30.3 %collective-permute-start.45 = (bf16[152,896]{1,0:T(8,128)(2,1)S(1)}, bf16[152,896]{1,0:T(8,128)(2,1)S(1)}, u32[]{:S(2)}, u32[]{:S(2)}) collective-permute-start(bf16[152,896]{1,0:T(8,128)(2,1)S(1)} %slice_bitcast_fusion.17), channel_id=1, source_target_pairs={{0,16},{1,17},{2,18},{3,19},{4,20},{5,21},{6,22},{7,23},{8,24},{9,... | collective-permute-start | bytes 817160 | tf_op jit(solution)/shard_map/ppermute | solution.py:90
  355.1 27.5 %collective-permute-start.38 = (bf16[2,64,384]{2,1,0:T(8,128)(2,1)S(1)}, bf16[2,64,384]{2,1,0:T(8,128)(2,1)S(1)}, u32[]{:S(2)}, u32[]{:S(2)}) collective-permute-start(bf16[2,64,384]{2,1,0:T(8,128)(2,1)S(1)} %dynamic-slice_bitcast_fusion.6), channel_id=1, source_target_pairs={{0,8},{1,9},{2,10},{3,11},{4,12},{5,13},{6,14},{7,15},{8,0},{9,1},... | collective-permute-start | bytes 294920 | tf_op jit(solution)/shard_map/ppermute | solution.py:90
  (72 other events, 488.0 us)
Sparse Core Ops, SparseCore 0:
  10.7 91.9 all-gather.2

commit v3 on v2

--- a/solution.py
+++ b/solution.py
@@ -90,8 +90,7 @@
     return lax.ppermute(value, "dp", [(i, i ^ (1 << bit)) for i in range(size)])
 
 
-def orders_of(size):
-    bits = list(range(1, bits_of(size)))
+def orders_of(bits):
     near, far = bits[:3], bits[3:]
     return tuple(near[i:] + near[:i] + far for i in range(3))
 
@@ -116,35 +115,70 @@
 def body(tokens, attn_weights, mlp_weights, norm_gains, qkv_bias, seq_lengths, cotangent):
     size = lax.axis_size("dp")
     index = lax.axis_index("dp")
-    core = index & 1
-    half = size // 2
-    same_core = [list(range(0, size, 2)), list(range(1, size, 2))]
-    orders = orders_of(size)
+    top = bits_of(size) - 1
+    quarter = size // 4
+    near_bits = list(range(1, top))
+    orders = orders_of(near_bits)
     num_rows = tokens.shape[0]
     attn_owned = attn_weights.shape[0]
     mlp_owned = mlp_weights.shape[0]
     kv_width = KV_HEADS * HEAD
 
-    attn_half = lax.all_gather(attn_weights, "dp", axis=0, axis_index_groups=same_core)
+    edges = (0, 384, 640, D)
+    attn_parts = [attn_weights[:, left:right] for left, right in zip(edges[:-1], edges[1:])]
+    attn_held = [[], [], []]
     pieces = [mlp_weights[:, i, :] for i in range(3)]
     held = [[], [], []]
-    steps = len(orders[0])
-    for step in range(steps):
-        if step:
-            pieces = start_together(pieces)
-        if step == steps - 1:
-            attn_half, *pieces = start_together([attn_half] + pieces)
+    steps = len(near_bits)
+
+    def widen_attn(step):
+        for i in range(3):
+            bit = (orders[i] + [top])[steps - step]
+            come = swap(attn_parts[i], size, bit)
+            first = ((index >> bit) & 1) == 0
+            attn_held[i] = sorted(attn_held[i] + [bit], reverse=True)
+            attn_parts[i] = jnp.stack(
+                [jnp.where(first, attn_parts[i], come), jnp.where(first, come, attn_parts[i])],
+                axis=attn_held[i].index(bit),
+            )
+
+    def widen_mlp(step):
         for i in range(3):
             bit = orders[i][steps - 1 - step]
             come = swap(pieces[i], size, bit)
             held[i] = sorted(held[i] + [bit], reverse=True)
             pieces[i] = jnp.stack([pieces[i], come], axis=held[i].index(bit))
-    w_gate, w_up, w_down = [piece.reshape(half * mlp_owned, D) for piece in pieces]
+
+    attn_parts = start_together(attn_parts)
+    widen_attn(0)
+    for step in range(steps):
+        together = start_together(attn_parts + pieces)
+        attn_parts, pieces = together[:3], together[3:]
+        widen_attn(step + 1)
+        if step < steps - 1:
+            widen_mlp(step)
+    attn_half = jnp.concatenate(
+        [part.reshape(size // 2, attn_owned, part.shape[-1]) for part in attn_parts], axis=2
+    )
+    attn_half, cotangent, *pieces = start_together([attn_half, cotangent] + pieces)
     attn_other = swap(attn_half, size, 0)
+    last_comes = [swap(pieces[i], size, orders[i][0]) for i in range(3)]
     attention = jnp.stack(
-        [jnp.where(core == 0, attn_half, attn_other), jnp.where(core == 0, attn_other, attn_half)],
+        [
+            jnp.where(index & 1 == 0, attn_half, attn_other),
+            jnp.where(index & 1 == 0, attn_other, attn_half),
+        ],
         axis=1,
     ).reshape(size * attn_owned, D)
+
+    def four_blocks(own):
+        far = swap(own, size, top)
+        return jnp.concatenate([own, swap(own, size, 0), far, swap(far, size, 0)], axis=0)
+
+    def back_to_owner(partial):
+        four = partial.reshape(2, 2, num_rows, D)
+        pair = four[:, 0] + swap(four[:, 1], size, 0)
+        return pair[0] + swap(pair[1].astype(jnp.bfloat16), size, top).astype(jnp.float32)
 
     segment, position, live = layout(seq_lengths[0], num_rows)
     slot_index = jnp.arange(num_rows, dtype=jnp.int32)
@@ -153,7 +187,7 @@
     inputs = tokens.astype(jnp.float32)
     upstream = cotangent.astype(jnp.float32) * live.astype(jnp.float32)[:, None]
     upstream_low = upstream.astype(jnp.bfloat16)
-    upstream_two = jnp.concatenate([upstream_low, swap(upstream_low, size, 0)], axis=0)
+    upstream_four = four_blocks(upstream_low)
 
     normed_one, inv_one = normalize(inputs, gains[0])
     normed_low = normed_one.astype(jnp.bfloat16)
@@ -166,6 +200,13 @@
         projected[:, D : D + kv_width].reshape(num_rows, KV_HEADS, HEAD), cosine, sine_table
     ).astype(jnp.bfloat16)
     value_low = projected[:, D + kv_width :].reshape(num_rows, KV_HEADS, HEAD).astype(jnp.bfloat16)
+    query_low, *last_comes = start_together([query_low] + last_comes)
+    w_gate, w_up, w_down = [
+        jnp.stack([pieces[i], last_comes[i]], axis=near_bits[::-1].index(orders[i][0])).reshape(
+            quarter * mlp_owned, D
+        )
+        for i in range(3)
+    ]
     query = query_low.reshape(num_rows, KV_HEADS, GROUP, HEAD)
     allowed = (segment[:, None] == segment[None, :]) & (slot_index[None, :] <= slot_index[:, None])
     raw_scores = jnp.einsum("qkgh,skh->kgqs", query, key_low, preferred_element_type=jnp.float32)
@@ -183,31 +224,29 @@
     normed_two, inv_two = normalize(hidden, gains[1])
     normed_two_low = normed_two.astype(jnp.bfloat16)
 
-    normed_pair = jnp.concatenate([normed_two_low, swap(normed_two_low, size, 0)], axis=0)
-    gate_proj = contract_last(normed_pair, w_gate)
-    up_proj = contract_last(normed_pair, w_up)
+    normed_four = four_blocks(normed_two_low)
+    gate_proj = contract_last(normed_four, w_gate)
+    up_proj = contract_last(normed_four, w_up)
     gate_sigmoid = jax.nn.sigmoid(gate_proj)
     active_low = (gate_proj * gate_sigmoid * up_proj).astype(jnp.bfloat16)
-    grad_active = contract_last(upstream_two, w_down)
+    grad_active = contract_last(upstream_four, w_down)
     grad_gate_low = (
         grad_active * up_proj * gate_sigmoid * (1.0 + gate_proj * (1.0 - gate_sigmoid))
     ).astype(jnp.bfloat16)
     grad_up_low = (grad_active * gate_proj * gate_sigmoid).astype(jnp.bfloat16)
-    back_pair = plain_dot(grad_gate_low, w_gate) + plain_dot(grad_up_low, w_up)
-    grad_normed_two = back_pair[:num_rows] + swap(back_pair[num_rows:], size, 0)
-    down_pair = plain_dot(active_low, w_down)
-    layer_out = (hidden + (down_pair[:num_rows] + swap(down_pair[num_rows:], size, 0))).astype(
-        jnp.bfloat16
-    )
-
-    all_bits = list(range(bits_of(size) - 1, 0, -1))
-    mlp_held = [list(all_bits) for _ in range(3)]
+    back_four = plain_dot(grad_gate_low, w_gate) + plain_dot(grad_up_low, w_up)
+    back_four, grad_gate_low, grad_up_low, active_low = start_together(
+        [back_four, grad_gate_low, grad_up_low, active_low]
+    )
+    grad_normed_two = back_to_owner(back_four)
+
+    mlp_held = [near_bits[::-1] for _ in range(3)]
     mlp_parts = [
-        split_rows(contract_first(left, right).astype(jnp.bfloat16), half, mlp_owned)
+        split_rows(contract_first(left, right).astype(jnp.bfloat16), quarter, mlp_owned)
         for left, right in (
-            (grad_gate_low, normed_pair),
-            (grad_up_low, normed_pair),
-            (active_low, upstream_two),
+            (grad_gate_low, normed_four),
+            (grad_up_low, normed_four),
+            (active_low, upstream_four),
         )
     ]
 
@@ -230,6 +269,8 @@
     grad_mid, grad_gain_two = norm_backward(hidden, gains[1], inv_two, grad_normed_two)
     grad_hidden = upstream + grad_mid
     grad_hidden_low = grad_hidden.astype(jnp.bfloat16)
+    grad_hidden_low, active_low = start_together([grad_hidden_low, active_low])
+    layer_out = (hidden + back_to_owner(plain_dot(active_low, w_down))).astype(jnp.bfloat16)
     grad_out_proj = contract_first(grad_hidden_low, attended_low).astype(jnp.bfloat16)
     grad_attended_low = plain_dot(grad_hidden_low, attention[QKV:]).astype(jnp.bfloat16)
     grad_part = grad_attended_low.reshape(num_rows, KV_HEADS, GROUP, HEAD)
@@ -257,6 +298,7 @@
         ],
         axis=1,
     ).astype(jnp.bfloat16)
+    grad_qkv_low, *first_comes = start_together([grad_qkv_low] + first_comes)
     grad_bias_term = jnp.sum(grad_qkv_low, axis=0, dtype=jnp.float32)
     grad_qkv_weights = contract_first(grad_qkv_low, normed_low).astype(jnp.bfloat16)
     grad_normed_one = plain_dot(grad_qkv_low, attention[:QKV])
@@ -264,16 +306,15 @@
     grad_tokens = grad_hidden + grad_input_mid
 
     attn_term = jnp.concatenate([grad_qkv_weights, grad_out_proj], axis=0)
-    edges = (0, 384, 640, D)
     attn_parts = [
         split_rows(attn_term[:, left:right], size, attn_owned)
         for left, right in zip(edges[:-1], edges[1:])
     ]
-    attn_orders = [[0] + order for order in orders]
-    attn_held = [list(all_bits) + [0] for _ in range(3)]
+    attn_orders = [[0] + order + [top] for order in orders]
+    attn_held = [list(range(top, -1, -1)) for _ in range(3)]
     small = jnp.concatenate([grad_gain_one, grad_gain_two, grad_bias_term])
     mlp_receive(0, first_comes)
-    for step in range(steps + 1):
+    for step in range(top + 1):
         sends, keeps = [], []
         for i in range(3):
             bit = attn_orders[i][step]
@@ -294,7 +335,7 @@
                 step + 1,
                 [swap(sends[4 + i], size, orders[i][step + 1]) for i in range(3)],
             )
-        attn_parts = [add_low(keeps[i], comes[i], step == steps) for i in range(3)]
+        attn_parts = [add_low(keeps[i], comes[i], step == top) for i in range(3)]
     grad_attn = jnp.concatenate(attn_parts, axis=1)
     grad_mlp = jnp.stack(mlp_parts, axis=1)
     grad_gains = small[: 2 * D].reshape(2, D)

time: 409 us -> 368 us (0.90); the launches traced: 400 us -> 364 us
  waiting for transfers between devices: 179 us -> 127 us
  starting transfers between devices: 50.7 us -> 68.8 us
  between operations: 15.3 us -> 2.3 us
  matrix products: 71 us -> 79.3 us
  local copies, waits for them, and re-layouts: 37.6 us -> 44.9 us
  other arithmetic: 47.2 us -> 42.2 us
    ppermute x49 -> x61, waiting for transfers between devices: 178 us -> 127 us  [swap(): return lax.ppermute(value, 'dp', [(i, i ^ 1 << bit) for i in range(size)])]
    ppermute x49 -> x61, starting transfers between devices: 50.7 us -> 68.8 us  [swap(): return lax.ppermute(value, 'dp', [(i, i ^ 1 << bit) for i in range(size)])]
    another operation x18 -> x38, other arithmetic: 20.3 us -> 13 us  [the longest x3 4.47 us: body(): jnp.stack([pieces[i], last_comes[i]], axis=near_bits[::-1].index(orders[i...]
    dot_general x0 -> x1, local copies, waits for them, and re-layouts: none -> 7.09 us  [plain_dot(): return jnp.dot(left, right, preferred_element_type=jnp.float32)]
    dot_general x5, matrix products: 22.6 us -> 28.2 us  [contract_last(): lax.dot_general(left, right, (((1,), (1,)), ((), ())), preferred_element_...]
    convert_element_type x21 -> x18, other arithmetic: 14.7 us -> 10.5 us  [add_low(): return total if last else total.astype(jnp.bfloat16)]
    unnamed x95 -> x131, local copies, waits for them, and re-layouts: 13.2 us -> 12.8 us
  transfers between devices with their start and end apart: 50 -> 61, of which waited for: 27 -> 27; matrix products, arithmetic and copies ran while one was open for 30% -> 31% of each run, Pallas kernels for 0% -> 0%
where the time goes in v3:
time: 368 us; the launch traced here: 364 us
  waiting for transfers between devices  127 us (35%)
  matrix products  79.3 us (22%)
  starting transfers between devices  68.8 us (19%)
  local copies, waits for them, and re-layouts  44.9 us (12%)
  other arithmetic  42.2 us (11%)
    ppermute x61, waiting for transfers between devices, swap(): return lax.ppermute(value, 'dp', [(i, i ^ 1 << bit) for i in range(size)])  127 us
    ppermute x61, starting transfers between devices, swap(): return lax.ppermute(value, 'dp', [(i, i ^ 1 << bit) for i in range(size)])  68.8 us
    dot_general x5, matrix products, contract_last(): lax.dot_general(left, right, (((1,), (1,)), ((), ())), preferred_element_...  28.2 us
    dot_general x5, matrix products, plain_dot(): return jnp.dot(left, right, preferred_element_type=jnp.float32)  15.2 us
    unnamed x131, local copies, waits for them, and re-layouts  12.8 us
    dot_general x5, matrix products, contract_first(): lax.dot_general(left, right, (((0,), (0,)), ((), ())), preferred_element_...  12.4 us
    convert_element_type x18, other arithmetic, add_low(): return total if last else total.astype(jnp.bfloat16)  10.5 us
  transfers between devices with their start and end apart: 61, of which 27 were waited for; matrix products, arithmetic and copies ran while one was open for 31% of the time, Pallas kernels for 0%

profile of v3, /device:TPU:0, one launch (start us, length us, event | category | flops | bytes accessed | tf_op | source)
XLA Modules:
  0.0 364.0 jit_solution(13281488206437776032)
XLA Ops:
  2.2 4.0 %collective-permute-start.2 = (bf16[64,256]{1,0:T(8,128)(2,1)S(1)}, bf16[64,256]{1,0:T(8,128)(2,1)S(1)}, u32[]{:S(2)}, u32[]{:S(2)}) collective-permute-start(bf16[64,256]{1,0:T(8,128)(2,1)S(1)} %get-tuple-element.74), channel_id=1, source_target_pairs={{0,16},{1,17},{2,18},{3,19},{4,20},{5,21},{6,22},{7,23},{8,24},{9,... | collective-permute-start | bytes 98312 | tf_op jit(solution)/shard_map/ppermute | solution.py:90
  32.6 8.5 %collective-permute-done.10 = bf16[2,2,64,256]{3,2,1,0:T(8,128)(2,1)S(1)} collective-permute-done((bf16[2,2,64,256]{3,2,1,0:T(8,128)(2,1)S(1)}, bf16[2,2,64,256]{3,2,1,0:T(8,128)(2,1)S(1)}, u32[]{:S(2)}, u32[]{:S(2)}) %collective-permute-start.10) | collective-permute-done | bytes 131104 | tf_op jit(solution)/shard_map/ppermute | solution.py:90
  58.9 3.1 collective-permute-start.23
  65.3 18.0 %collective-permute-done.23 = bf16[256,896]{1,0:T(8,128)(2,1)} collective-permute-done((bf16[256,896]{1,0:T(8,128)(2,1)}, bf16[256,896]{1,0:T(8,128)(2,1)}, u32[]{:S(2)}, u32[]{:S(2)}) %collective-permute-start.23) | collective-permute-done | bytes 458784 | tf_op jit(solution)/shard_map/ppermute | solution.py:90
  93.4 16.1 %collective-permute-done.21 = bf16[2,2,152,896]{3,2,0,1:T(8,128)(2,1)} collective-permute-done((bf16[2,2,152,896]{3,2,0,1:T(8,128)(2,1)}, bf16[2,2,152,896]{3,2,0,1:T(8,128)(2,1)}, u32[]{:S(2)}, u32[]{:S(2)}) %collective-permute-start.21) | collective-permute-done | bytes 1089568 | tf_op jit(solution)/shard_map/ppermute | solution.py:90
  110.0 3.1 fusion.90
  124.0 15.0 %collective-permute-done.26 = bf16[256,896]{1,0:T(8,128)(2,1)S(1)} collective-permute-done((bf16[256,896]{1,0:T(8,128)(2,1)S(1)}, bf16[256,896]{1,0:T(8,128)(2,1)S(1)}, u32[]{:S(2)}, u32[]{:S(2)}) %collective-permute-start.26) | collective-permute-done | bytes 458784 | tf_op jit(solution)/shard_map/ppermute | solution.py:90
  139.0 15.8 %fusion.61 = f32[1024,1216]{0,1:T(8,128)S(1)} fusion(bf16[1216,896]{1,0:T(8,128)(2,1)S(1)} %bitcast.446, bf16[256,896]{1,0:T(8,128)(2,1)} %collective-permute-done.24, bf16[256,896]{1,0:T(8,128)(2,1)} %collective-permute-done.23, bf16[256,896]{1,0:T(8,128)(2,1)} %collective-permute-done.22, bf16[256,896]{1,0:T(8,128)(2,1)} %fusion.47), kind=kOutput, calls=%fused_computation.169 | convolution fusion | flops 2238709760 | bytes 8994816 | tf_op jit(solution)/shard_map/dot_general | solution.py:70
  157.7 7.8 %multiply_convert_fusion = (bf16[1024,1216]{0,1:T(8,128)(2,1)}, bf16[1024,1216]{0,1:T(8,128)(2,1)S(1)}, bf16[1024,1216]{0,1:T(8,128)(2,1)S(1)}) fusion(f32[1024,1216]{0,1:T(8,128)S(1)} %fusion.84, f32[1024,1216]{0,1:T(8,128)S(1)} %fusion.61, bf16[1216,896]{1,0:T(8,128)(2,1)S(1)} %bitcast.450, bf16[256,896]{1,0:T(8,128)(2,1)S(1)} %collective-permute-done.27, ...), kind=kOutput, calls=%fused_computation.2 | convolution fusion | flops 2258632704 | bytes 21446656 | tf_op jit(solution)/shard_map/dot_general | solution.py:70
  165.4 3.0 fusion.91
  168.5 3.0 convolution_add_fusion.1
  175.0 4.9 %convolution_convert_fusion = bf16[1216,896]{1,0:T(8,128)(2,1)S(1)} fusion(bf16[1024,1216]{0,1:T(8,128)(2,1)} %get-tuple-element.104, bf16[256,896]{1,0:T(8,128)(2,1)} %collective-permute-done.24, bf16[256,896]{1,0:T(8,128)(2,1)} %collective-permute-done.23, bf16[256,896]{1,0:T(8,128)(2,1)} %collective-permute-done.22, bf16[256,896]{1,0:T(8,128)(2,1)} %fusion.47), kind=kOutput, calls=%fused_computation.19 | convolution fusion | flops 2239799296 | bytes 6504448 | tf_op jit(solution)/shard_map/dot_general | solution.py:76
  192.0 3.2 convolution_convert_fusion.2
  199.6 16.6 %collective-permute-done.29 = bf16[256,896]{1,0:T(8,128)(2,1)S(1)} collective-permute-done((bf16[256,896]{1,0:T(8,128)(2,1)S(1)}, bf16[256,896]{1,0:T(8,128)(2,1)S(1)}, u32[]{:S(2)}, u32[]{:S(2)}) %collective-permute-start.29) | collective-permute-done | bytes 458784 | tf_op jit(solution)/shard_map/ppermute | solution.py:90
  222.7 3.4 fusion.92
  226.1 6.6 %fusion.19 = f32[2,64,7,256]{3,1,2,0:T(8,128)S(1)} fusion(bf16[256,2,64,1]{0,2,3,1:T(8,128)(2,1)S(1)} %copy-done.44, f32[2,256,256,7]{2,1,3,0:T(8,128)} %fusion.92, f32[2,7,256,256]{2,3,1,0:T(8,128)} %get-tuple-element.207, f32[2,7,256]{2,1,0:T(8,128)S(1)} %get-tuple-element.206), kind=kOutput, calls=%fused_computation.63 | convolution fusion | flops 123866880 | bytes 8337408 | tf_op jit(solution)/shard_map/kgqs,skh->qkgh/dot_general | solution.py:285
  232.7 7.3 %broadcast_multiply_fusion = (f32[256,2,64]{0,2,1:T(8,128)}, f32[256,2,64]{0,2,1:T(8,128)}) fusion(f32[256,64]{0,1:T(8,128)S(1)} %copy-done.31, bf16[256,2,7,64]{0,3,2,1:T(8,128)(2,1)S(1)} %bitcast.472, f32[2,256,256,7]{2,1,3,0:T(8,128)} %fusion.92, f32[2,7,256,256]{2,3,1,0:T(8,128)} %get-tuple-element.207, f32[2,7,256]{2,1,0:T(8,128)S(1)} %get-tuple-element.206), kind=kOutput, calls=%fused_computation.235 | convolution fusion | flops 123899648 | bytes 8140800 | tf_op jit(solution)/shard_map/kgqs,qkgh->skh/dot_general | solution.py:288
  264.9 3.4 collective-permute-start.40
  268.8 7.1 %dot_general.74 = bf16[2,2,256,1216]{2,1,0,3:T(2,128)(2,1)} reshape(bf16[1024,1216]{0,1:T(8,128)(2,1)} %get-tuple-element.104) | data formatting | bytes 4980736 | tf_op jit(solution)/shard_map/dot_general | solution.py:82
  275.9 5.3 %fusion.6 = f32[2,2,256,896]{3,2,0,1:T(8,128)S(1)} fusion(bf16[1216,896,1,1]{1,0,2,3:T(8,128)(2,1)} %bitcast.447, bf16[2,2,256,1216]{2,1,0,3:T(2,128)(2,1)} %dot_general.74), kind=kOutput, calls=%fused_computation.25 | convolution fusion | flops 2231369728 | bytes 8339456 | tf_op jit(solution)/shard_map/dot_general | solution.py:82
  291.5 6.6 %collective-permute-done.39 = bf16[2,152,896]{2,1,0:T(8,128)(2,1)S(1)} collective-permute-done((bf16[2,152,896]{2,1,0:T(8,128)(2,1)S(1)}, bf16[2,152,896]{2,1,0:T(8,128)(2,1)S(1)}, u32[]{:S(2)}, u32[]{:S(2)}) %collective-permute-start.39) | collective-permute-done | bytes 544800 | tf_op jit(solution)/shard_map/ppermute | solution.py:90
  316.2 3.3 collective-permute-done.58
  324.7 3.0 collective-permute-done.46
  350.6 12.3 %collective-permute-done.31 = bf16[256,896]{1,0:T(8,128)(2,1)S(1)} collective-permute-done((bf16[256,896]{1,0:T(8,128)(2,1)S(1)}, bf16[256,896]{1,0:T(8,128)(2,1)S(1)}, u32[]{:S(2)}, u32[]{:S(2)}) %collective-permute-start.31) | collective-permute-done | bytes 458784 | tf_op jit(solution)/shard_map/ppermute | solution.py:90
  (411 shorter events, 181.5 us)
Async XLA Ops:
  27.5 15.7 %collective-permute-start.14 = (bf16[2,152,896]{2,1,0:T(8,128)(2,1)S(1)}, bf16[2,152,896]{2,1,0:T(8,128)(2,1)S(1)}, u32[]{:S(2)}, u32[]{:S(2)}) collective-permute-start(bf16[2,152,896]{2,1,0:T(8,128)(2,1)S(1)} %pad_maximum_fusion.17), channel_id=1, source_target_pairs={{0,2},{1,3},{2,0},{3,1},{4,6},{5,7},{6,4},{7,5},{8,10},{9,11},{10,... | collective-permute-start | bytes 1634312 | tf_op jit(solution)/shard_map/ppermute | solution.py:90
  28.1 16.3 %collective-permute-start.13 = (bf16[2,152,896]{2,1,0:T(8,128)(2,1)S(1)}, bf16[2,152,896]{2,1,0:T(8,128)(2,1)S(1)}, u32[]{:S(2)}, u32[]{:S(2)}) collective-permute-start(bf16[2,152,896]{2,1,0:T(8,128)(2,1)S(1)} %pad_maximum_fusion.16), channel_id=1, source_target_pairs={{0,8},{1,9},{2,10},{3,11},{4,12},{5,13},{6,14},{7,15},{8,0},{9,1},... | collective-permute-start | bytes 1634312 | tf_op jit(solution)/shard_map/ppermute | solution.py:90
  29.3 16.2 %collective-permute-start.12 = (bf16[2,152,896]{2,1,0:T(8,128)(2,1)S(1)}, bf16[2,152,896]{2,1,0:T(8,128)(2,1)S(1)}, u32[]{:S(2)}, u32[]{:S(2)}) collective-permute-start(bf16[2,152,896]{2,1,0:T(8,128)(2,1)S(1)} %pad_maximum_fusion.15), channel_id=1, source_target_pairs={{0,4},{1,5},{2,6},{3,7},{4,0},{5,1},{6,2},{7,3},{8,12},{9,13},{10,... | collective-permute-start | bytes 1634312 | tf_op jit(solution)/shard_map/ppermute | solution.py:90
  56.6 26.8 %collective-permute-start.18 = (bf16[16,64,896]{2,1,0:T(8,128)(2,1)S(1)}, bf16[16,64,896]{2,1,0:T(8,128)(2,1)}, u32[]{:S(2)}, u32[]{:S(2)}) collective-permute-start(bf16[16,64,896]{2,1,0:T(8,128)(2,1)S(1)} %pad_maximum_fusion.3), channel_id=1, source_target_pairs={{0,1},{1,0},{2,3},{3,2},{4,5},{5,4},{6,7},{7,6},{8,9},{9,8},{10,11... | collective-permute-start | bytes 5505032 | tf_op jit(solution)/shard_map/ppermute | solution.py:90
  58.9 24.4 %collective-permute-start.23 = (bf16[256,896]{1,0:T(8,128)(2,1)}, bf16[256,896]{1,0:T(8,128)(2,1)}, u32[]{:S(2)}, u32[]{:S(2)}) collective-permute-start(bf16[256,896]{1,0:T(8,128)(2,1)} %fusion.47), channel_id=1, source_target_pairs={{0,16},{1,17},{2,18},{3,19},{4,20},{5,21},{6,22},{7,23},{8,24},{9,... | collective-permute-start | bytes 1376264 | tf_op jit(solution)/shard_map/ppermute | solution.py:90
  63.4 75.6 %collective-permute-start.22 = (bf16[256,896]{1,0:T(8,128)(2,1)}, bf16[256,896]{1,0:T(8,128)(2,1)}, u32[]{:S(2)}, u32[]{:S(2)}) collective-permute-start(bf16[256,896]{1,0:T(8,128)(2,1)} %fusion.47), channel_id=1, source_target_pairs={{0,1},{1,0},{2,3},{3,2},{4,5},{5,4},{6,7},{7,6},{8,9},{9,8},{10,11... | collective-permute-start | bytes 1376264 | tf_op jit(solution)/shard_map/ppermute | solution.py:90
  63.5 29.8 %collective-permute-start.19 = (bf16[2,2,152,896]{3,2,1,0:T(8,128)(2,1)}, bf16[2,2,152,896]{3,2,1,0:T(8,128)(2,1)}, u32[]{:S(2)}, u32[]{:S(2)}) collective-permute-start(bf16[2,2,152,896]{3,2,1,0:T(8,128)(2,1)} %pad_maximum_fusion.8), channel_id=1, source_target_pairs={{0,2},{1,3},{2,0},{3,1},{4,6},{5,7},{6,4},{7,5},{8,10},{9,11},{10,... | collective-permute-start | bytes 3268616 | tf_op jit(solution)/shard_map/ppermute | solution.py:90
  64.6 28.7 %collective-permute-start.20 = (bf16[2,2,152,896]{3,2,1,0:T(8,128)(2,1)}, bf16[2,2,152,896]{3,2,1,0:T(8,128)(2,1)}, u32[]{:S(2)}, u32[]{:S(2)}) collective-permute-start(bf16[2,2,152,896]{3,2,1,0:T(8,128)(2,1)} %pad_maximum_fusion.9), channel_id=1, source_target_pairs={{0,4},{1,5},{2,6},{3,7},{4,0},{5,1},{6,2},{7,3},{8,12},{9,13},{10,... | collective-permute-start | bytes 3268616 | tf_op jit(solution)/shard_map/ppermute | solution.py:90
  83.3 26.2 %collective-permute-start.21 = (bf16[2,2,152,896]{3,2,0,1:T(8,128)(2,1)}, bf16[2,2,152,896]{3,2,0,1:T(8,128)(2,1)}, u32[]{:S(2)}, u32[]{:S(2)}) collective-permute-start(bf16[2,2,152,896]{3,2,0,1:T(8,128)(2,1)} %pad_maximum_fusion.10), channel_id=1, source_target_pairs={{0,8},{1,9},{2,10},{3,11},{4,12},{5,13},{6,14},{7,15},{8,0},{9,1},... | collective-permute-start | bytes 3268616 | tf_op jit(solution)/shard_map/ppermute | solution.py:90
  83.3 55.6 %collective-permute-start.24 = (bf16[256,896]{1,0:T(8,128)(2,1)}, bf16[256,896]{1,0:T(8,128)(2,1)}, u32[]{:S(2)}, u32[]{:S(2)}) collective-permute-start(bf16[256,896]{1,0:T(8,128)(2,1)} %collective-permute-done.23), channel_id=1, source_target_pairs={{0,1},{1,0},{2,3},{3,2},{4,5},{5,4},{6,7},{7,6},{8,9},{9,8},{10,11... | collective-permute-start | bytes 1376264 | tf_op jit(solution)/shard_map/ppermute | solution.py:90
  116.6 22.3 %collective-permute-start.26 = (bf16[256,896]{1,0:T(8,128)(2,1)S(1)}, bf16[256,896]{1,0:T(8,128)(2,1)S(1)}, u32[]{:S(2)}, u32[]{:S(2)}) collective-permute-start(bf16[256,896]{1,0:T(8,128)(2,1)S(1)} %multiply_convert_fusion.3), channel_id=1, source_target_pairs={{0,16},{1,17},{2,18},{3,19},{4,20},{5,21},{6,22},{7,23},{8,24},{9,... | collective-permute-start | bytes 1376264 | tf_op jit(solution)/shard_map/ppermute | solution.py:90
  117.9 36.9 %collective-permute-start.25 = (bf16[256,896]{1,0:T(8,128)(2,1)S(1)}, bf16[256,896]{1,0:T(8,128)(2,1)S(1)}, u32[]{:S(2)}, u32[]{:S(2)}) collective-permute-start(bf16[256,896]{1,0:T(8,128)(2,1)S(1)} %multiply_convert_fusion.3), channel_id=1, source_target_pairs={{0,1},{1,0},{2,3},{3,2},{4,5},{5,4},{6,7},{7,6},{8,9},{9,8},{10,11... | collective-permute-start | bytes 1376264 | tf_op jit(solution)/shard_map/ppermute | solution.py:90
  138.9 15.9 %collective-permute-start.27 = (bf16[256,896]{1,0:T(8,128)(2,1)S(1)}, bf16[256,896]{1,0:T(8,128)(2,1)S(1)}, u32[]{:S(2)}, u32[]{:S(2)}) collective-permute-start(bf16[256,896]{1,0:T(8,128)(2,1)S(1)} %collective-permute-done.26), channel_id=1, source_target_pairs={{0,1},{1,0},{2,3},{3,2},{4,5},{5,4},{6,7},{7,6},{8,9},{9,8},{10,11... | collective-permute-start | bytes 1376264 | tf_op jit(solution)/shard_map/ppermute | solution.py:90
  182.2 61.6 %collective-permute-start.34 = (bf16[2,2,152,896]{3,2,0,1:T(8,128)(2,1)}, bf16[2,2,152,896]{3,2,0,1:T(8,128)(2,1)}, u32[]{:S(2)}, u32[]{:S(2)}) collective-permute-start(bf16[2,2,152,896]{3,2,0,1:T(8,128)(2,1)} %copy.112), channel_id=1, source_target_pairs={{0,8},{1,9},{2,10},{3,11},{4,12},{5,13},{6,14},{7,15},{8,0},{9,1},... | collective-permute-start | bytes 3268616 | tf_op jit(solution)/shard_map/ppermute | solution.py:90
  187.0 56.8 %collective-permute-start.33 = (bf16[2,2,152,896]{3,2,1,0:T(8,128)(2,1)}, bf16[2,2,152,896]{3,2,1,0:T(8,128)(2,1)}, u32[]{:S(2)}, u32[]{:S(2)}) collective-permute-start(bf16[2,2,152,896]{3,2,1,0:T(8,128)(2,1)} %slice_bitcast_fusion.5), channel_id=1, source_target_pairs={{0,4},{1,5},{2,6},{3,7},{4,0},{5,1},{6,2},{7,3},{8,12},{9,13},{10,... | collective-permute-start | bytes 3268616 | tf_op jit(solution)/shard_map/ppermute | solution.py:90
  189.5 26.6 %collective-permute-start.29 = (bf16[256,896]{1,0:T(8,128)(2,1)S(1)}, bf16[256,896]{1,0:T(8,128)(2,1)S(1)}, u32[]{:S(2)}, u32[]{:S(2)}) collective-permute-start(bf16[256,896]{1,0:T(8,128)(2,1)S(1)} %fusion.56), channel_id=1, source_target_pairs={{0,16},{1,17},{2,18},{3,19},{4,20},{5,21},{6,22},{7,23},{8,24},{9,... | collective-permute-start | bytes 1376264 | tf_op jit(solution)/shard_map/ppermute | solution.py:90
  197.5 46.4 %collective-permute-start.32 = (bf16[2,2,152,896]{3,2,0,1:T(8,128)(2,1)}, bf16[2,2,152,896]{3,2,0,1:T(8,128)(2,1)}, u32[]{:S(2)}, u32[]{:S(2)}) collective-permute-start(bf16[2,2,152,896]{3,2,0,1:T(8,128)(2,1)} %bitcast.423), channel_id=1, source_target_pairs={{0,2},{1,3},{2,0},{3,1},{4,6},{5,7},{6,4},{7,5},{8,10},{9,11},{10,... | collective-permute-start | bytes 3268616 | tf_op jit(solution)/shard_map/ppermute | solution.py:90
  264.0 25.0 %collective-permute-start.41 = (bf16[2,152,896]{2,1,0:T(8,128)(2,1)}, bf16[2,152,896]{2,1,0:T(8,128)(2,1)}, u32[]{:S(2)}, u32[]{:S(2)}) collective-permute-start(bf16[2,152,896]{2,1,0:T(8,128)(2,1)} %slice_bitcast_fusion.11), channel_id=1, source_target_pairs={{0,2},{1,3},{2,0},{3,1},{4,6},{5,7},{6,4},{7,5},{8,10},{9,11},{10,... | collective-permute-start | bytes 1634312 | tf_op jit(solution)/shard_map/ppermute | solution.py:90
  264.9 25.3 %collective-permute-start.40 = (bf16[2,152,896]{2,1,0:T(8,128)(2,1)}, bf16[2,152,896]{2,1,0:T(8,128)(2,1)}, u32[]{:S(2)}, u32[]{:S(2)}) collective-permute-start(bf16[2,152,896]{2,1,0:T(8,128)(2,1)} %slice_bitcast_fusion.12), channel_id=1, source_target_pairs={{0,8},{1,9},{2,10},{3,11},{4,12},{5,13},{6,14},{7,15},{8,0},{9,1},... | collective-permute-start | bytes 1634312 | tf_op jit(solution)/shard_map/ppermute | solution.py:90
  268.3 17.5 %collective-permute-start.37 = (bf16[2,2,2,2,64,256]{5,4,0,2,3,1:T(8,128)(2,1)}, bf16[2,2,2,2,64,256]{5,4,0,2,3,1:T(8,128)(2,1)}, u32[]{:S(2)}, u32[]{:S(2)}) collective-permute-start(bf16[2,2,2,2,64,256]{5,4,0,2,3,1:T(8,128)(2,1)} %bitcast.425), channel_id=1, source_target_pairs={{0,1},{1,0},{2,3},{3,2},{4,5},{5,4},{6,7},{7,6},{8,9},{9,8},{10,11... | collective-permute-start | bytes 1572872 | tf_op jit(solution)/shard_map/ppermute | solution.py:90
  268.8 18.5 %collective-permute-start.36 = (bf16[2,2,2,2,64,256]{5,4,0,3,1,2:T(8,128)(2,1)}, bf16[2,2,2,2,64,256]{5,4,0,3,1,2:T(8,128)(2,1)}, u32[]{:S(2)}, u32[]{:S(2)}) collective-permute-start(bf16[2,2,2,2,64,256]{5,4,0,3,1,2:T(8,128)(2,1)} %bitcast.426), channel_id=1, source_target_pairs={{0,1},{1,0},{2,3},{3,2},{4,5},{5,4},{6,7},{7,6},{8,9},{9,8},{10,11... | collective-permute-start | bytes 1572872 | tf_op jit(solution)/shard_map/ppermute | solution.py:90
  287.3 56.0 %collective-permute-start.30 = (f32[2,256,896]{2,1,0:T(8,128)}, f32[2,256,896]{2,1,0:T(8,128)}, u32[]{:S(2)}, u32[]{:S(2)}) collective-permute-start(f32[2,256,896]{2,1,0:T(8,128)} %slice_bitcast_fusion), channel_id=1, source_target_pairs={{0,1},{1,0},{2,3},{3,2},{4,5},{5,4},{6,7},{7,6},{8,9},{9,8},{10,11... | collective-permute-start | bytes 5505032 | tf_op jit(solution)/shard_map/ppermute | solution.py:90
  310.0 19.2 %collective-permute-start.59 = (bf16[152,896]{1,0:T(8,128)(2,1)S(1)}, bf16[152,896]{1,0:T(8,128)(2,1)S(1)}, u32[]{:S(2)}, u32[]{:S(2)}) collective-permute-start(bf16[152,896]{1,0:T(8,128)(2,1)S(1)} %slice_bitcast_fusion.17), channel_id=1, source_target_pairs={{0,4},{1,5},{2,6},{3,7},{4,0},{5,1},{6,2},{7,3},{8,12},{9,13},{10,... | collective-permute-start | bytes 817160 | tf_op jit(solution)/shard_map/ppermute | solution.py:90
  345.6 17.2 %collective-permute-start.31 = (bf16[256,896]{1,0:T(8,128)(2,1)S(1)}, bf16[256,896]{1,0:T(8,128)(2,1)S(1)}, u32[]{:S(2)}, u32[]{:S(2)}) collective-permute-start(bf16[256,896]{1,0:T(8,128)(2,1)S(1)} %fusion.57), channel_id=1, source_target_pairs={{0,16},{1,17},{2,18},{3,19},{4,20},{5,21},{6,22},{7,23},{8,24},{9,... | collective-permute-start | bytes 1376264 | tf_op jit(solution)/shard_map/ppermute | solution.py:90
  (103 other events, 1058.0 us)
